TPU v7x, 256 devices: a whole 4x4x8 slice. The times are simulated.
256 devices in a mesh: col: 64 (over z, y, core), row: 4 (over x).
Axes of the slice: x: 4, y: 4, z: 8, core: 2. Of those that a mesh axis runs over, the one named last changes fastest.
Arguments:
- diag_blocks: float32 [128, 512, 512], P('col'), may hold values from -1 to 3, as said below
- panel_blocks: float32 [128, 8, 512, 512], P('col', None, 'row'), may hold values from -0.3 to 0.3
- ancestors: int32 [128, 8], P('col'), may hold values from 0 to 63, all different within a row; in each aligned block of 2 rows (0 to 1, 2 to 3, ...) at most 2 rows name the same one
- target_ids: int32 [64], P('col'), may hold values from 0 to 63, each once
- target_tiles: float32 [64, 512, 512], P('col', 'row'), may hold values from -6 to 6
Outputs:
- panel_factor: float32 [128, 8, 512, 512], P('col', None, 'row')
- updated_tiles: float32 [64, 512, 512], P('col', 'row')
Inputs may be any that keep to these rules, and one draw needn't show every extreme that they name: `ancestors`: each row names 8 different target blocks; on the supernodes of one index of col a target block is named at most twice, and exactly twice somewhere; every target block is named. `target_ids`: A permutation of the target blocks. `diag_blocks`: each block is symmetric and positive definite, with smallest eigenvalue 0.05 or more.
All inputs are finite; a program needn't handle non-finite values.
Results may differ from a plain program's by a relative error of at most 0.0029.
Values may be sent and summed in bfloat16 or wider, within the bound.
No kernel may reach another device: no remote copies, remote signals or barrier semaphores. Data moves between devices by JAX's collectives and lax.ppermute only.
A program may use at most 128 MiB of HBM per device.

v0:
```python
import functools

import jax
import jax.numpy as jnp
from jax import lax
from jax.experimental import pallas as pl
from jax.experimental.pallas import tpu as pltpu
from jax.sharding import Mesh, PartitionSpec as P

F32 = jnp.float32
BF16 = jnp.bfloat16
BLK = 128
FIRST = 256
PAN = 16
FIRST_LIMIT = 48 * 1024 * 1024
VMEM_LIMIT = 24 * 1024 * 1024
SMALL_LIMIT = 8 * 1024 * 1024
COL = ("z", "y", "core")
COST = pl.CostEstimate(flops=10**6, bytes_accessed=10**4, transcendentals=0)


def split3(x):
    a = x.astype(BF16)
    rest = x - a.astype(F32)
    b = rest.astype(BF16)
    c = (rest - b.astype(F32)).astype(BF16)
    return a, b, c


def split2(x):
    a = x.astype(BF16)
    return a, (x - a.astype(F32)).astype(BF16)


def outer_product(left, right):
    a, b, c = split3(left)
    p, q, r = split3(right)
    return lax.dot_general(
        jnp.concatenate([a, a, a, b, b, c], axis=0),
        jnp.concatenate([p, q, r, p, q, p], axis=0),
        (((0,), (0,)), ((), ())),
        preferred_element_type=F32,
    )


def dot_dims(a, b, dims, precision=None):
    return lax.dot_general(a, b, (dims, ((), ())), precision=precision, preferred_element_type=F32)


def refined_reciprocal(d):
    r = pl.reciprocal(d, approx=True)
    r = r * (2.0 - d * r)
    return r * (2.0 - d * r)


def factor_panel(panel, k):
    half = PAN // 2
    lane1 = lax.broadcasted_iota(jnp.int32, (1, BLK), 1)
    sub = lax.broadcasted_iota(jnp.int32, (half, BLK), 0)
    lane = lax.broadcasted_iota(jnp.int32, (half, BLK), 1)
    top, bot = panel[:half], panel[half:]
    tops = [jnp.broadcast_to(top[:, k + c : k + c + 1], (half, BLK)) for c in range(PAN)]
    bots = [jnp.broadcast_to(bot[:, k + c : k + c + 1], (half, BLK)) for c in range(PAN)]
    diag_top = jnp.ones((half, BLK), F32)
    diag_bot = jnp.ones((half, BLK), F32)
    for i in range(PAN):
        if i < half:
            d = tops[i][i : i + 1]
            r = refined_reciprocal(d)
            mt = jnp.where(sub > i, tops[i] * r, 0.0)
            mb = bots[i] * r
            diag_top = jnp.where(sub == i, d, diag_top)
            for c in range(i + 1, PAN):
                row = tops[c][i : i + 1]
                tops[c] = tops[c] - mt * row
                bots[c] = bots[c] - mb * row
            pivot = top[i : i + 1] + jnp.where(lane1 == k + i, 1.0, 0.0)
            top = top - mt * pivot
            bot = bot - mb * pivot
        else:
            h = i - half
            d = bots[i][h : h + 1]
            r = refined_reciprocal(d)
            mb = jnp.where(sub > h, bots[i] * r, 0.0)
            diag_bot = jnp.where(sub == h, d, diag_bot)
            for c in range(i + 1, PAN):
                bots[c] = bots[c] - mb * bots[c][h : h + 1]
            pivot = bot[h : h + 1] + jnp.where(lane1 == k + i, 1.0, 0.0)
            bot = bot - mb * pivot

    def finish(rows, diag, first):
        at = lane - k - first
        rows = jnp.where(at == sub, 1.0, jnp.where((at > sub) & (lane < k + PAN), 0.0, rows))
        return rows * lax.rsqrt(diag)

    return jnp.concatenate([finish(top, diag_top, 0), finish(bot, diag_bot, half)], axis=0)


def factor_blocks(blocks):
    mats = list(blocks)
    done = [[] for _ in mats]
    for k in range(0, BLK, PAN):
        lane = lax.broadcasted_iota(jnp.int32, (PAN, BLK), 1)
        for s in range(len(mats)):
            rows = factor_panel(mats[s][:PAN], k)
            done[s].append(jnp.where(lane < k + PAN, rows, 0.0))
            if k + PAN < BLK:
                ahead = jnp.where(lane >= k + PAN, rows, 0.0)
                rest = mats[s][PAN:]
                at = lax.broadcasted_iota(jnp.int32, rest.shape, 1)
                rest = jnp.where((at >= k) & (at < k + PAN), 0.0, rest)
                mats[s] = rest - outer_product(ahead, rows)[k + PAN :]
    return [jnp.concatenate(rows, axis=0) for rows in done]


def factor_rows(k, s, row, w_prev):
    if not k:
        return row
    lane = lax.broadcasted_iota(jnp.int32, row.shape, 1)
    left = jnp.concatenate([w[:, BLK * k : BLK * (k + 1)] for w in w_prev], axis=0)
    right = jnp.concatenate(
        [jnp.where((lane >= BLK * (i + 1)) & (lane < BLK * k), 0.0, w) for i, w in enumerate(w_prev)],
        axis=0,
    )
    row = jnp.where(lane < BLK * k, 0.0, row)
    return row - dot_dims(left, right, ((0,), (0,)), lax.Precision.HIGHEST)


def factor_part(first, sn, diag_ref, *refs):
    w_ref = refs[-1]
    width = diag_ref.shape[2]
    w_prev = [
        [w[s, BLK * i : BLK * (i + 1), :] for w in refs[:-1] for i in range(w.shape[1] // BLK)]
        for s in range(sn)
    ]
    for at in range(diag_ref.shape[1] // BLK):
        k = first + at
        here = slice(BLK * k, BLK * (k + 1))
        rows = [
            factor_rows(k, s, diag_ref[s, BLK * at : BLK * (at + 1), :], w_prev[s]) for s in range(sn)
        ]
        inverses = factor_blocks([row[:, here] for row in rows])
        for s in range(sn):
            scaled = dot_dims(inverses[s], rows[s], ((1,), (0,)), lax.Precision.HIGHEST)
            lane = lax.broadcasted_iota(jnp.int32, (BLK, width), 1)
            inside = (lane >= BLK * k) & (lane < BLK * (k + 1))
            spread = jnp.concatenate([inverses[s]] * (width // BLK), axis=1)
            scaled = jnp.where(inside, spread, scaled)
            w_prev[s].append(scaled)
            w_ref[s, BLK * at : BLK * (at + 1), :] = scaled


def solve_part(start, stop, sn, info_ref, w_ref, b_ref, x_ref, r_refs, half_ref):
    tile = 256
    nt = ((1,), (1,))
    for s in range(sn):
        lane = lax.broadcasted_iota(jnp.int32, (stop - start, stop), 1)
        row = lax.broadcasted_iota(jnp.int32, (stop - start, stop), 0) + start
        w_hi, w_lo = split2(jnp.where(lane <= row, w_ref[s, :, :stop], 0.0))

        def step(t, carry):
            at = pl.ds(pl.multiple_of(t * tile, tile), tile)
            b_hi, b_lo = split2(b_ref[s, at, :])
            x = dot_dims(b_hi, w_hi, nt) + (dot_dims(b_hi, w_lo, nt) + dot_dims(b_lo, w_hi, nt))
            x_ref[s, at, :] = x
            r_refs[s][at, :] = x.astype(BF16)
            return carry

        lax.fori_loop(0, b_ref.shape[1] // tile, step, 0, unroll=True)
    chosen = jnp.where(info_ref[0] < 2, r_refs[1][...], r_refs[0][...])
    half_ref[...] = chosen


def first_kernel(sn, info_ref, diag_ref, b_hbm, w_ref, x_ref, r_ref, half_ref, b_ref, sem):
    copy = pltpu.make_async_copy(b_hbm.at[:, :, pl.ds(0, FIRST)], b_ref, sem)
    copy.start()
    factor_part(0, sn, diag_ref, w_ref)
    copy.wait()
    r_refs = [r_ref.at[s] for s in range(sn)]
    solve_part(0, FIRST, sn, info_ref, w_ref, b_ref, x_ref, r_refs, half_ref)


def second_kernel(sn, info_ref, w_ref, own_ref, b_ref, *refs):
    x_ref, r_ref, half_ref, product_ref, packed_ref = refs[2:]
    r_refs = [r_ref.at[s] for s in range(sn)]
    solve_part(FIRST, b_ref.shape[2], sn, info_ref, w_ref, b_ref, x_ref, r_refs, half_ref)
    anc = b_ref.shape[1] // BLK
    for s in range(sn):

        def square(c, carry):
            at = pl.ds(pl.multiple_of(c * BLK, BLK), BLK)
            mine = jnp.concatenate([own_ref[s * anc + c], r_refs[s][at, :]], axis=1)
            product = dot_dims(mine, mine, ((1,), (1,)))
            product_ref[s * anc + c] = product
            packed_ref[s * anc + c] = pack(product)
            return carry

        lax.fori_loop(0, anc, square, 0, unroll=4)


def whole(shape):
    return pl.BlockSpec(shape, lambda i: (0,) * len(shape))


def grid_call(kernel, args, in_specs, outs, name, scratch, limit, aliases={}):
    return pl.pallas_call(
        kernel,
        grid=(1,),
        in_specs=in_specs,
        out_specs=[spec for spec, _ in outs],
        out_shape=[shape for _, shape in outs],
        scratch_shapes=list(scratch),
        input_output_aliases=aliases,
        compiler_params=pltpu.CompilerParams(vmem_limit_bytes=limit),
        cost_estimate=COST,
        name=name,
    )(*args)


SMEM_SPEC = pl.BlockSpec(memory_space=pltpu.SMEM)
ANY_SPEC = pl.BlockSpec(memory_space=pl.ANY)


def first_chunk(row, diag_blocks, panel):
    sn, rows, width = panel.shape
    return grid_call(
        functools.partial(first_kernel, sn),
        [row, diag_blocks, panel],
        [SMEM_SPEC, pl.BlockSpec((sn, FIRST, width), lambda i: (0, 0, 0)), ANY_SPEC],
        [
            (whole((sn, FIRST, width)), f32_out(sn, FIRST, width)),
            (pl.BlockSpec((sn, rows, FIRST), lambda i: (0, 0, 0)), f32_out(sn, rows, width)),
            (whole((sn, rows, FIRST)), bf16_out(sn, rows, FIRST)),
            (whole((rows, FIRST)), bf16_out(rows, FIRST)),
        ],
        "first_chunk",
        [pltpu.VMEM((sn, rows, FIRST), F32), pltpu.SemaphoreType.DMA],
        FIRST_LIMIT,
    )


def second_factor(diag_blocks, w):
    sn, _, width = diag_blocks.shape
    return grid_call(
        functools.partial(factor_part, FIRST // BLK, sn),
        [diag_blocks, w],
        [pl.BlockSpec((sn, FIRST, width), lambda i: (0, 1, 0)), whole(w.shape)],
        [(whole(w.shape), f32_out(*w.shape))],
        "second_factor",
        [],
        VMEM_LIMIT,
    )[0]


def second_chunk(row, w, own, panel, solved, dep):
    sn, rows, width = panel.shape
    count = own.shape[0]
    return grid_call(
        functools.partial(second_kernel, sn),
        [row, w, own, panel, solved, dep],
        [SMEM_SPEC, whole(w.shape), whole(own.shape), whole(panel.shape), ANY_SPEC, ANY_SPEC],
        [
            (pl.BlockSpec((sn, rows, FIRST), lambda i: (0, 0, 1)), f32_out(sn, rows, width)),
            (whole((sn, rows, FIRST)), bf16_out(sn, rows, FIRST)),
            (whole((rows, FIRST)), bf16_out(rows, FIRST)),
            (whole((count, BLK, BLK)), f32_out(count, BLK, BLK)),
            (whole((count, BLK, BLK)), bf16_out(count, BLK, BLK)),
        ],
        "second_chunk",
        [],
        VMEM_LIMIT,
        {4: 0},
    )


def call(kernel, args, out_shape, scratch=(), name=None, smem=1, deps=(), through=()):
    n_args, n_more = len(args), len(deps) + len(through)
    n_outs = len(out_shape)
    specs = [SMEM_SPEC] * smem
    specs += [pl.BlockSpec(memory_space=pltpu.VMEM)] * (n_args - smem)

    def body(*refs):
        outs = refs[n_args + n_more : n_args + n_more + n_outs]
        kernel(*refs[:n_args], *outs, *refs[n_args + n_more + n_outs + len(through) :])

    return pl.pallas_call(
        body,
        in_specs=specs + [ANY_SPEC] * n_more,
        out_specs=[pl.BlockSpec(memory_space=pltpu.VMEM)] * n_outs + [ANY_SPEC] * len(through),
        out_shape=list(out_shape) + [jax.ShapeDtypeStruct(t.shape, t.dtype) for t in through],
        scratch_shapes=list(scratch),
        input_output_aliases={n_args + len(deps) + i: n_outs + i for i in range(len(through))},
        compiler_params=pltpu.CompilerParams(vmem_limit_bytes=SMALL_LIMIT),
        cost_estimate=COST,
        name=name,
    )(*args, *deps, *through)


def products_kernel(n, info_ref, *refs):
    own, right, across, (right_ref, across_ref) = refs[:n], refs[n : 2 * n], refs[2 * n : -2], refs[-2:]
    half = across_ref.shape[0]
    nt = ((1,), (1,))
    for s in range(2):

        def joined(group, c):
            return jnp.concatenate([r[s * half + c] for r in group], axis=1)

        def step(c, carry):
            right_ref[s * half + c] = dot_dims(joined(own, c), joined(right, c), nt)
            return carry

        def step_across(c, carry):
            other = jnp.concatenate([r[c] for r in across], axis=1)
            across_ref[c] = dot_dims(joined(own, c), other, nt)
            return carry

        lax.fori_loop(0, half, step, 0, unroll=4)

        @pl.when((info_ref[0] < 2) == (s == 0))
        def _():
            lax.fori_loop(0, half, step_across, 0, unroll=4)


def pack(block):
    lane = lax.broadcasted_iota(jnp.int32, (BLK, BLK), 1)
    row = lax.broadcasted_iota(jnp.int32, (BLK, BLK), 0)
    first = block
    hi = first.astype(BF16).astype(F32)
    rest = jnp.sum(jnp.where(lane == row, first - hi, 0.0), axis=1, keepdims=True)
    first = jnp.where(lane > row, 0.0, first)
    first = jnp.where(lane == row + 1, rest, first)
    last = jnp.sum(jnp.where((lane == row) & (row == BLK - 1), block - hi, 0.0), keepdims=True)
    first = jnp.where((row == 0) & (lane == BLK - 1), last, first)
    return first.astype(BF16)


def unpack(block):
    lane = lax.broadcasted_iota(jnp.int32, (BLK, BLK), 1)
    row = lax.broadcasted_iota(jnp.int32, (BLK, BLK), 0)
    first = block.astype(F32)
    last = jnp.sum(jnp.where((row == 0) & (lane == BLK - 1), first, 0.0), keepdims=True)
    rest = jnp.sum(jnp.where(lane == row + 1, first, 0.0), axis=1, keepdims=True)
    rest = jnp.where((row == BLK - 1), last, rest)
    first = jnp.where(lane == row, first + rest, first)
    first = jnp.where(lane > row, 0.0, first)
    return first


def known_kernel(info_ref, id_ref, names_ref, out_ref):
    me = info_ref[4]
    count = names_ref.shape[0]
    per = BLK // count
    lane = lax.broadcasted_iota(jnp.int32, out_ref.shape, 1)
    row = lax.broadcasted_iota(jnp.int32, out_ref.shape, 0)
    table = jnp.where((row == 0) & (lane == id_ref[0]), me, 0)
    mine = row == 1 + lax.div(me, per)
    for c in range(count):
        table = jnp.where(mine & (lane == lax.rem(me, per) * count + c), names_ref[c], table)
    out_ref[...] = table


def add_blocks(info_ref, known_ref, names, ref, acc, lanes, widen=lambda block: block):
    core = info_ref[0]

    def add(c, carry):
        p = known_ref[0, names(c)]

        @pl.when(lax.rem(p, 2) == core)
        def _():
            at = lax.div(p, 2)
            acc[at, :, lanes] += widen(ref[c])

        return carry

    lax.fori_loop(0, ref.shape[0], add, 0)


def name_tables(info_ref, known_ref, names_ref, count):
    other = info_ref[4] + 1 - 2 * info_ref[0]
    per = BLK // count
    return [
        lambda c: names_ref[c],
        lambda c: known_ref[1 + lax.div(other, per), lax.rem(other, per) * count + c],
    ]


def emit_y(ny, y, acc, own_ref, sends, narrow):
    def emit(z, carry):
        for d in range(ny):
            block = acc[z * ny + lax.rem(y + d, ny)]
            if d == 0:
                own_ref[z] = block
            else:
                sends[d - 1][z] = narrow(block)
        return carry

    lax.fori_loop(0, own_ref.shape[0], emit, 0)


def scatter_diag_kernel(ny, info_ref, known_ref, names_ref, mine_ref, theirs_ref, own_ref, *rest):
    sends, acc = rest[:-1], rest[-1]
    acc[...] = jnp.zeros_like(acc)
    mine, theirs = name_tables(info_ref, known_ref, names_ref, names_ref.shape[0])
    add_blocks(info_ref, known_ref, mine, mine_ref, acc, slice(None))
    add_blocks(info_ref, known_ref, theirs, theirs_ref, acc, slice(None), unpack)
    emit_y(ny, info_ref[1], acc, own_ref, sends, pack)


def scatter_off_kernel(ny, info_ref, known_ref, names_ref, *refs):
    (mine_ref, across_ref, theirs_ref, their_across_ref, own_ref), rest = refs[:5], refs[5:]
    sends, acc = rest[:-1], rest[-1]
    first = jnp.where(info_ref[3] < 2, 0, across_ref.shape[0])
    acc[...] = jnp.zeros_like(acc)
    tables = name_tables(info_ref, known_ref, names_ref, names_ref.shape[0])
    blocks = ((mine_ref, across_ref), (theirs_ref, their_across_ref))
    for names, (right, across) in zip(tables, blocks):
        add_blocks(info_ref, known_ref, names, right, acc, slice(0, BLK))
        add_blocks(info_ref, known_ref, lambda c: names(first + c), across, acc, slice(BLK, 2 * BLK))
    emit_y(ny, info_ref[1], acc, own_ref, sends, lambda block: block.astype(BF16))


def sum_y_kernel(diag, info_ref, own_ref, *refs):
    got, (out_ref, send_ref) = refs[:-2], refs[-2:]
    widen = unpack if diag else lambda block: block.astype(F32)
    narrow = pack if diag else lambda block: block.astype(BF16)

    def step(at, carry):
        total = own_ref[at]
        for ref in got:
            total += widen(ref[at])
        send_ref[at] = narrow(total)

        @pl.when(at == info_ref[2])
        def _():
            out_ref[...] = total

        return carry

    lax.fori_loop(0, own_ref.shape[0], step, 0)


def sum_z_kernel(info_ref, own_ref, got_ref, *out_refs):
    total = own_ref[...]
    for at in range(got_ref.shape[0]):
        total += jnp.where(info_ref[2] == at, 0.0, got_ref[at].astype(F32))
    for b, ref in enumerate(out_refs):
        ref[...] = total[:, BLK * b : BLK * (b + 1)]


def finish_kernel(info_ref, tile_ref, diag_ref, got_ref, right_ref, across_ref, left_in, across_in, out_ref):
    row, n = info_ref[3], 4
    r = lax.broadcasted_iota(jnp.int32, (BLK, BLK), 0)
    c = lax.broadcasted_iota(jnp.int32, (BLK, BLK), 1)
    low = diag_ref[...]
    for at in range(got_ref.shape[0]):
        low += jnp.where(info_ref[2] == at, 0.0, unpack(got_ref[at]))

    def put(at, value):
        cols = pl.ds(pl.multiple_of(at * BLK, BLK), BLK)
        out_ref[:, cols] = tile_ref[:, cols] - value

    put(row, jnp.where(c > r, low.T, low))
    put(lax.rem(row + 1, n), right_ref[...])
    put(lax.rem(row + 3, n), left_in[...].T)
    put(lax.rem(row + 2, n), across_ref[...] + across_in[...].T)


def ring(n, d):
    return [(i, (i + d) % n) for i in range(n)]


def f32_out(*shape):
    return jax.ShapeDtypeStruct(shape, F32)


def bf16_out(*shape):
    return jax.ShapeDtypeStruct(shape, BF16)


def on_device(diag_blocks, panel_blocks, ancestors, target_ids, target_tiles):
    nz, ny = lax.axis_size("z"), lax.axis_size("y")
    sn, anc, rows, width = panel_blocks.shape
    count = sn * anc
    half = count // sn
    z, y, core, row = (lax.axis_index(a).astype(jnp.int32) for a in ("z", "y", "core", "row"))
    info = jnp.stack([core, y, z, row, (z * ny + y) * 2 + core])
    at_row = row[None]
    panel = panel_blocks.reshape(sn, anc * rows, width)
    names = ancestors.reshape(count)

    def send(blocks, distance):
        return lax.ppermute(blocks, "row", ring(4, distance))

    def blocks(part):
        return part.reshape(-1, rows, part.shape[-1])

    def after_scatter(kernel, args, wide, name, **kwargs):
        return call(
            functools.partial(kernel, ny),
            [info, known, names, *args],
            [f32_out(nz, BLK, wide)] + [bf16_out(nz, BLK, wide)] * (ny - 1),
            [pltpu.VMEM((nz * ny, BLK, wide), F32)],
            name=name,
            smem=3,
            **kwargs,
        )

    def along_y(sends):
        return [lax.ppermute(s, "y", ring(ny, d + 1)) for d, s in enumerate(sends)]

    def sum_y(own, got, name, deps=(), diag=False):
        wide = own.shape[2]
        outs = [f32_out(BLK, wide), bf16_out(nz, BLK, wide)]
        kernel = functools.partial(sum_y_kernel, diag)
        own, sends = call(kernel, [info, own, *got], outs, name=name, deps=deps)
        return own, lax.all_to_all(sends, "z", 0, 0, tiled=True)

    w, solved, rounded, part = first_chunk(at_row, diag_blocks, panel)
    own = [blocks(rounded)]
    right = [send(own[0], -1)]
    hop = send(blocks(part), 1)
    w = second_factor(diag_blocks, w)
    solved, rounded, part, diag, packed = second_chunk(at_row, w, own[0], panel, solved, hop)
    own.append(blocks(rounded))
    right.append(send(own[1], -1))
    across = [send(hop, 1), send(blocks(part), 2)]
    their_diag = lax.ppermute(packed, "core", ring(2, 1))

    (known,) = call(
        known_kernel,
        [info, target_ids, names],
        [jax.ShapeDtypeStruct((1 + nz * ny * 2 * count // BLK, BLK), jnp.int32)],
        name="known",
        smem=3,
        deps=[diag, right[0]],
    )
    known = lax.psum(known, COL)
    own_diag, *sends = after_scatter(scatter_diag_kernel, [diag, their_diag], BLK, "scatter_diag")
    got_diag = along_y(sends)
    off_right, off_across = call(
        functools.partial(products_kernel, len(own)),
        [at_row, *own, *right, *across],
        [f32_out(count, BLK, BLK), f32_out(half, BLK, BLK)],
        name="products",
        deps=got_diag,
    )
    their_right = lax.ppermute(off_right, "core", ring(2, 1))
    their_across = lax.ppermute(off_across, "core", ring(2, 1))
    own_off, *sends = after_scatter(
        scatter_off_kernel, [off_right, off_across, their_right, their_across], 2 * BLK, "scatter_off"
    )
    got_off = along_y(sends)
    own_diag, got_diag = sum_y(own_diag, got_diag, "sum_diag", [own_off], diag=True)
    own_off, got_off = sum_y(own_off, got_off, "sum_off", [got_diag])
    off_right, off_across = call(
        sum_z_kernel, [info, own_off, got_off], [f32_out(BLK, BLK)] * 2, name="last_sum"
    )
    from_left = send(off_right, 1)
    from_across = send(off_across, 2)
    (updated,) = call(
        finish_kernel,
        [info, target_tiles.reshape(rows, width), own_diag, got_diag]
        + [off_right, off_across, from_left, from_across],
        [f32_out(rows, width)],
        name="finish",
    )
    return solved.reshape(panel_blocks.shape), updated.reshape(target_tiles.shape)


def solution(mesh):
    devices = mesh.devices
    nz, ny = 8, 4
    fine = Mesh(devices.reshape(nz, ny, 2, devices.shape[1]), ("z", "y", "core", "row"))
    in_specs = (
        P(COL, None, None),
        P(COL, None, "row", None),
        P(COL, None),
        P(COL),
        P(COL, "row", None),
    )
    out_specs = (P(COL, None, "row", None), P(COL, "row", None))
    return jax.shard_map(
        on_device, mesh=fine, in_specs=in_specs, out_specs=out_specs, check_vma=False
    )
```

profile of v0, /device:TPU:26, one launch (start us, length us, event | category | flops | bytes accessed | tf_op | source)
XLA Modules:
  0.0 156.5 jit_solution(9348774281746483522)
XLA Ops:
  0.6 1.6 %copy-done.1 = f32[2,512,512]{2,1,0:T(8,128)S(1)} copy-done((f32[2,512,512]{2,1,0:T(8,128)S(1)}, f32[2,512,512]{2,1,0:T(8,128)}, u32[]{:S(2)}) %copy-start.1) | copy-done | bytes 2097176
  2.2 14.0 %first_chunk.1 = (f32[2,256,512]{2,1,0:T(8,128)S(1)}, f32[2,1024,512]{2,1,0:T(8,128)}, bf16[2,1024,256]{2,1,0:T(8,128)(2,1)S(1)}, bf16[1024,256]{1,0:T(8,128)(2,1)S(1)}) custom-call(s32[1]{0:T(128)} %bitcast.info_ref.refs_0_, f32[2,512,512]{2,1,0:T(8,128)S(1)} %copy-done.1, f32[2,1024,512]{2,1,0:T(8,128)} %bitcast.13), custom_call_target="tpu_custom_call" | custom-call | flops 1000000 | bytes 10000 | tf_op jit(solution)/shard_map/first_chunk/pallas_call | solution.py:206
  16.2 1.6 %collective-permute-start = (bf16[8,128,256]{2,1,0:T(8,128)(2,1)S(1)}, bf16[8,128,256]{2,1,0:T(8,128)(2,1)}, u32[]{:S(2)}, u32[]{:S(2)}) collective-permute-start(bf16[8,128,256]{2,1,0:T(8,128)(2,1)S(1)} %bitcast.19), channel_id=1, source_target_pairs={{0,1},{1,2},{2,3},{3,0},{4,5},{5,6},{6,7},{7,4},{8,9},{9,10},{10,1... | collective-permute-start | bytes 1572872 | tf_op jit(solution)/shard_map/ppermute | solution.py:492
  17.8 0.5 collective-permute-start.1
  18.3 11.6 %second_factor.1.w_ref = f32[2,256,512]{2,1,0:T(8,128)S(1)} custom-call(f32[2,512,512]{2,1,0:T(8,128)S(1)} %copy-done.1, f32[2,256,512]{2,1,0:T(8,128)S(1)} %get-tuple-element.27.refs_0_), custom_call_target="tpu_custom_call" | custom-call | flops 1000000 | bytes 10000 | tf_op jit(solution)/shard_map/second_factor/pallas_call | solution.py:206
  29.9 0.2 collective-permute-done.refs_1_
  30.1 5.3 %second_chunk.1 = (f32[2,1024,512]{2,1,0:T(8,128)}, bf16[2,1024,256]{2,1,0:T(8,128)(2,1)}, bf16[1024,256]{1,0:T(8,128)(2,1)}, f32[16,128,128]{2,1,0:T(8,128)S(1)}, bf16[16,128,128]{2,1,0:T(8,128)(2,1)}) custom-call(s32[1]{0:T(128)} %bitcast.info_ref.refs_0_, f32[2,256,512]{2,1,0:T(8,128)S(1)} %second_factor.1.w_ref, ...), custom_call_target="tpu_custom_call", output_to_operand_aliasing={{0}: (4, {})} | custom-call | flops 1000000 | bytes 10000 | tf_op jit(solution)/shard_map/second_chunk/pallas_call | solution.py:206
  35.4 1.7 %collective-permute-start.6 = (bf16[16,128,256]{2,1,0:T(8,128)(2,1)}, bf16[16,128,256]{2,1,0:T(8,128)(2,1)}, u32[]{:S(2)}, u32[]{:S(2)}) collective-permute-start(bf16[16,128,256]{2,1,0:T(8,128)(2,1)} %bitcast.10.refs_2_), channel_id=1, source_target_pairs={{0,3},{1,0},{2,1},{3,2},{4,7},{5,4},{6,5},{7,6},{8,11},{9,8},{10,9... | collective-permute-start | bytes 3145736 | tf_op jit(solution)/shard_map/ppermute | solution.py:492
  37.2 0.0 collective-permute-start.2
  37.2 1.2 collective-permute-start.8
  38.4 1.8 %collective-permute-start.7 = (bf16[8,128,256]{2,1,0:T(8,128)(2,1)}, bf16[8,128,256]{2,1,0:T(8,128)(2,1)}, u32[]{:S(2)}, u32[]{:S(2)}) collective-permute-start(bf16[8,128,256]{2,1,0:T(8,128)(2,1)} %collective-permute-done.refs_1_), channel_id=1, source_target_pairs={{0,1},{1,2},{2,3},{3,0},{4,5},{5,6},{6,7},{7,4},{8,9},{9,10},{10,1... | collective-permute-start | bytes 1572872 | tf_op jit(solution)/shard_map/ppermute | solution.py:492
  40.2 0.1 reshape.36.refs_2_
  40.9 0.1 stack.20.refs_0_
  41.0 2.9 %collective-permute-done.1.refs_4_.refs_3_ = bf16[16,128,256]{2,1,0:T(8,128)(2,1)S(1)} collective-permute-done((bf16[16,128,256]{2,1,0:T(8,128)(2,1)S(1)}, bf16[16,128,256]{2,1,0:T(8,128)(2,1)S(1)}, u32[]{:S(2)}, u32[]{:S(2)}) %collective-permute-start.1) | collective-permute-done | bytes 1048608 | tf_op jit(solution)/shard_map/ppermute | solution.py:492
  43.9 0.6 known.1
  44.5 21.9 %psum.7.refs_1_ = s32[9,128]{1,0:T(8,128)S(1)} all-reduce(s32[9,128]{1,0:T(8,128)S(1)} %known.1), channel_id=1, replica_groups=mesh['z'=8,'y'=4,'core'=2,'row'=4] {'z','y','core'}, use_global_device_ids=true, to_apply=%region_0.0 | all-reduce | flops 1152 | bytes 9216 | tf_op jit(solution)/shard_map/psum | solution.py:537
  66.4 0.0 collective-permute-done.2.refs_4_
  66.4 4.0 %scatter_diag.1 = (f32[8,128,128]{2,1,0:T(8,128)S(1)}, bf16[8,128,128]{2,1,0:T(8,128)(2,1)S(1)}, bf16[8,128,128]{2,1,0:T(8,128)(2,1)S(1)}, bf16[8,128,128]{2,1,0:T(8,128)(2,1)S(1)}) custom-call(s32[5]{0:T(128)S(1)} %stack.20.refs_0_, s32[9,128]{1,0:T(8,128)S(1)} %psum.7.refs_1_, s32[16]{0:T(128)S(1)} %reshape.36.refs_2_, ...), custom_call_target="tpu_custom_call" | custom-call | flops 1000000 | bytes 10000 | tf_op jit(solution)/shard_map/scatter_diag/pallas_call | solution.py:286
  70.4 2.8 %collective-permute-start.3 = (bf16[8,128,128]{2,1,0:T(8,128)(2,1)S(1)}, bf16[8,128,128]{2,1,0:T(8,128)(2,1)S(1)}, u32[]{:S(2)}, u32[]{:S(2)}) collective-permute-start(bf16[8,128,128]{2,1,0:T(8,128)(2,1)S(1)} %get-tuple-element.35), channel_id=1, source_target_pairs={{0,8},{8,16},{16,24},{24,0},{1,9},{9,17},{17,25},{25,1},{2,10},{10... | collective-permute-start | bytes 786440 | tf_op jit(solution)/shard_map/ppermute | solution.py:509
  73.2 0.2 collective-permute-start.4
  73.4 3.5 %collective-permute-done.8.refs_6_ = bf16[8,128,256]{2,1,0:T(8,128)(2,1)} collective-permute-done((bf16[8,128,256]{2,1,0:T(8,128)(2,1)}, bf16[8,128,256]{2,1,0:T(8,128)(2,1)}, u32[]{:S(2)}, u32[]{:S(2)}) %collective-permute-start.8) | collective-permute-done | bytes 524320 | tf_op jit(solution)/shard_map/ppermute | solution.py:492
  76.9 0.7 collective-permute-start.5
  77.6 3.6 %collective-permute-done.3.refs_7_.refs_2_ = bf16[8,128,128]{2,1,0:T(8,128)(2,1)S(1)} collective-permute-done((bf16[8,128,128]{2,1,0:T(8,128)(2,1)S(1)}, bf16[8,128,128]{2,1,0:T(8,128)(2,1)S(1)}, u32[]{:S(2)}, u32[]{:S(2)}) %collective-permute-start.3) | collective-permute-done | bytes 262176 | tf_op jit(solution)/shard_map/ppermute | solution.py:509
  81.2 2.1 %collective-permute-done.4.refs_8_.refs_3_ = bf16[8,128,128]{2,1,0:T(8,128)(2,1)S(1)} collective-permute-done((bf16[8,128,128]{2,1,0:T(8,128)(2,1)S(1)}, bf16[8,128,128]{2,1,0:T(8,128)(2,1)S(1)}, u32[]{:S(2)}, u32[]{:S(2)}) %collective-permute-start.4) | collective-permute-done | bytes 262176 | tf_op jit(solution)/shard_map/ppermute | solution.py:509
  83.3 3.9 %collective-permute-done.5.refs_9_.refs_4_ = bf16[8,128,128]{2,1,0:T(8,128)(2,1)S(1)} collective-permute-done((bf16[8,128,128]{2,1,0:T(8,128)(2,1)S(1)}, bf16[8,128,128]{2,1,0:T(8,128)(2,1)S(1)}, u32[]{:S(2)}, u32[]{:S(2)}) %collective-permute-start.5) | collective-permute-done | bytes 262176 | tf_op jit(solution)/shard_map/ppermute | solution.py:509
  87.2 0.0 collective-permute-done.6.refs_4_
  87.2 3.6 %products.1 = (f32[16,128,128]{2,1,0:T(8,128)S(1)}, f32[8,128,128]{2,1,0:T(8,128)S(1)}) custom-call(s32[1]{0:T(128)} %bitcast.info_ref.refs_0_, bf16[16,128,256]{2,1,0:T(8,128)(2,1)S(1)} %bitcast.17, bf16[16,128,256]{2,1,0:T(8,128)(2,1)} %bitcast.10.refs_2_, bf16[16,128,256]{2,1,0:T(8,128)(2,1)S(1)} %collective-permute-done.1.refs_4_.refs_3_, ...), custom_call_target="tpu_custom_call" | custom-call | flops 1000000 | bytes 10000 | tf_op jit(solution)/shard_map/products/pallas_call | solution.py:286
  90.8 0.1 collective-permute-start.9
  90.9 0.5 collective-permute-start.10
  91.4 2.9 %collective-permute-done.10.refs_6_ = f32[8,128,128]{2,1,0:T(8,128)S(1)} collective-permute-done((f32[8,128,128]{2,1,0:T(8,128)S(1)}, f32[8,128,128]{2,1,0:T(8,128)S(1)}, u32[]{:S(2)}, u32[]{:S(2)}) %collective-permute-start.10) | collective-permute-done | bytes 524320 | tf_op jit(solution)/shard_map/ppermute | solution.py:548
  94.3 0.0 collective-permute-done.9.refs_5_
  94.3 2.4 %scatter_off.1 = (f32[8,128,256]{2,1,0:T(8,128)S(1)}, bf16[8,128,256]{2,1,0:T(8,128)(2,1)S(1)}, bf16[8,128,256]{2,1,0:T(8,128)(2,1)S(1)}, bf16[8,128,256]{2,1,0:T(8,128)(2,1)S(1)}) custom-call(s32[5]{0:T(128)S(1)} %stack.20.refs_0_, s32[9,128]{1,0:T(8,128)S(1)} %psum.7.refs_1_, s32[16]{0:T(128)S(1)} %reshape.36.refs_2_, ...), custom_call_target="tpu_custom_call" | custom-call | flops 1000000 | bytes 10000 | tf_op jit(solution)/shard_map/scatter_off/pallas_call | solution.py:286
  96.8 0.0 copy-start.2
  96.8 0.1 collective-permute-start.11
  96.9 0.3 collective-permute-start.12
  97.1 1.8 %collective-permute-start.13 = (bf16[8,128,256]{2,1,0:T(8,128)(2,1)S(1)}, bf16[8,128,256]{2,1,0:T(8,128)(2,1)S(1)}, u32[]{:S(2)}, u32[]{:S(2)}) collective-permute-start(bf16[8,128,256]{2,1,0:T(8,128)(2,1)S(1)} %get-tuple-element.47), channel_id=1, source_target_pairs={{0,24},{8,0},{16,8},{24,16},{1,25},{9,1},{17,9},{25,17},{2,26},{10... | collective-permute-start | bytes 1572872 | tf_op jit(solution)/shard_map/ppermute | solution.py:509
  98.9 2.6 %sum_diag.1 = (f32[128,128]{1,0:T(8,128)S(1)}, bf16[8,128,128]{2,1,0:T(8,128)(2,1)S(1)}) custom-call(s32[5]{0:T(128)S(1)} %stack.20.refs_0_, f32[8,128,128]{2,1,0:T(8,128)S(1)} %get-tuple-element.34.refs_1_, bf16[8,128,128]{2,1,0:T(8,128)(2,1)S(1)} %collective-permute-done.3.refs_7_.refs_2_, bf16[8,128,128]{2,1,0:T(8,128)(2,1)S(1)} %collective-permute-done.4.refs_8_.refs_3_, ...), custom_call_target="tpu_custom_call" | custom-call | flops 1000000 | bytes 10000 | tf_op jit(solution)/shard_map/sum_diag/pallas_call | solution.py:286
  101.5 17.7 %all_to_all.10.refs_5_.refs_3_ = bf16[8,128,128]{2,1,0:T(8,128)(2,1)S(1)} all-to-all(bf16[8,128,128]{2,1,0:T(8,128)(2,1)S(1)} %get-tuple-element.44), channel_id=1, replica_groups=mesh['z'=8,'y'=4,'core'=2,'row'=4] {'z'}, dimensions={0} | all-to-all | bytes 524288 | tf_op jit(solution)/shard_map/all_to_all | solution.py:516
  119.1 0.0 collective-permute-done.11.refs_2_
  119.1 4.6 %collective-permute-done.13.refs_4_ = bf16[8,128,256]{2,1,0:T(8,128)(2,1)S(1)} collective-permute-done((bf16[8,128,256]{2,1,0:T(8,128)(2,1)S(1)}, bf16[8,128,256]{2,1,0:T(8,128)(2,1)S(1)}, u32[]{:S(2)}, u32[]{:S(2)}) %collective-permute-start.13) | collective-permute-done | bytes 524320 | tf_op jit(solution)/shard_map/ppermute | solution.py:509
  123.7 0.8 sum_off.1
  124.6 23.7 %all_to_all.11.refs_2_ = bf16[8,128,256]{2,1,0:T(8,128)(2,1)S(1)} all-to-all(bf16[8,128,256]{2,1,0:T(8,128)(2,1)S(1)} %get-tuple-element.49), channel_id=1, replica_groups=mesh['z'=8,'y'=4,'core'=2,'row'=4] {'z'}, dimensions={0} | all-to-all | bytes 1048576 | tf_op jit(solution)/shard_map/all_to_all | solution.py:516
  148.2 0.7 last_sum.1
  148.9 0.1 collective-permute-start.14
  149.0 1.5 collective-permute-start.15
  150.5 2.7 %collective-permute-done.14.refs_6_ = f32[128,128]{1,0:T(8,128)S(1)} collective-permute-done((f32[128,128]{1,0:T(8,128)S(1)}, f32[128,128]{1,0:T(8,128)S(1)}, u32[]{:S(2)}, u32[]{:S(2)}) %collective-permute-start.14) | collective-permute-done | bytes 65568 | tf_op jit(solution)/shard_map/ppermute | solution.py:492
  153.2 1.6 %collective-permute-done.15.refs_7_ = f32[128,128]{1,0:T(8,128)S(1)} collective-permute-done((f32[128,128]{1,0:T(8,128)S(1)}, f32[128,128]{1,0:T(8,128)S(1)}, u32[]{:S(2)}, u32[]{:S(2)}) %collective-permute-start.15) | collective-permute-done | bytes 65568 | tf_op jit(solution)/shard_map/ppermute | solution.py:492
  154.8 1.6 %finish.1 = f32[128,512]{1,0:T(8,128)} custom-call(s32[5]{0:T(128)S(1)} %stack.20.refs_0_, f32[128,512]{1,0:T(8,128)S(1)} %bitcast.18, f32[128,128]{1,0:T(8,128)S(1)} %get-tuple-element.43.refs_2_, bf16[8,128,128]{2,1,0:T(8,128)(2,1)S(1)} %all_to_all.10.refs_5_.refs_3_, f32[128,128]{1,0:T(8,128)S(1)} %get-tuple-element.50.refs_4_, ...), custom_call_target="tpu_custom_call" | custom-call | flops 1000000 | bytes 10000 | tf_op jit(solution)/shard_map/finish/pallas_call | solution.py:286
  (8 shorter events, 0.0 us)
Async XLA Ops:
  0.6 1.6 %copy-start.1 = (f32[2,512,512]{2,1,0:T(8,128)S(1)}, f32[2,512,512]{2,1,0:T(8,128)}, u32[]{:S(2)}) copy-start(f32[2,512,512]{2,1,0:T(8,128)} %diag_ref.3) | copy-start | bytes 6291460
  2.2 27.9 %copy-start = (f32[2,8,128,512]{3,2,1,0:T(8,128)S(1)}, f32[2,8,128,512]{3,2,1,0:T(8,128)}, u32[]{:S(2)}) copy-start(f32[2,8,128,512]{3,2,1,0:T(8,128)} %param.6) | copy-start | bytes 12582916
  16.2 13.8 %collective-permute-start = (bf16[8,128,256]{2,1,0:T(8,128)(2,1)S(1)}, bf16[8,128,256]{2,1,0:T(8,128)(2,1)}, u32[]{:S(2)}, u32[]{:S(2)}) collective-permute-start(bf16[8,128,256]{2,1,0:T(8,128)(2,1)S(1)} %bitcast.19), channel_id=1, source_target_pairs={{0,1},{1,2},{2,3},{3,0},{4,5},{5,6},{6,7},{7,4},{8,9},{9,10},{10,1... | collective-permute-start | bytes 1572872 | tf_op jit(solution)/shard_map/ppermute | solution.py:492
  17.8 26.1 %collective-permute-start.1 = (bf16[16,128,256]{2,1,0:T(8,128)(2,1)S(1)}, bf16[16,128,256]{2,1,0:T(8,128)(2,1)S(1)}, u32[]{:S(2)}, u32[]{:S(2)}) collective-permute-start(bf16[16,128,256]{2,1,0:T(8,128)(2,1)S(1)} %bitcast.15), channel_id=1, source_target_pairs={{0,3},{1,0},{2,1},{3,2},{4,7},{5,4},{6,5},{7,6},{8,11},{9,8},{10,9... | collective-permute-start | bytes 3145736 | tf_op jit(solution)/shard_map/ppermute | solution.py:492
  30.1 10.1 %copy-start.3 = (s32[2,8]{1,0:T(2,128)S(1)}, s32[2,8]{1,0:T(2,128)}, u32[]{:S(2)}) copy-start(s32[2,8]{1,0:T(2,128)} %param.7) | copy-start | bytes 196
  35.4 51.8 %collective-permute-start.6 = (bf16[16,128,256]{2,1,0:T(8,128)(2,1)}, bf16[16,128,256]{2,1,0:T(8,128)(2,1)}, u32[]{:S(2)}, u32[]{:S(2)}) collective-permute-start(bf16[16,128,256]{2,1,0:T(8,128)(2,1)} %bitcast.10.refs_2_), channel_id=1, source_target_pairs={{0,3},{1,0},{2,1},{3,2},{4,7},{5,4},{6,5},{7,6},{8,11},{9,8},{10,9... | collective-permute-start | bytes 3145736 | tf_op jit(solution)/shard_map/ppermute | solution.py:492
  37.2 29.2 %collective-permute-start.2 = (bf16[16,128,128]{2,1,0:T(8,128)(2,1)}, bf16[16,128,128]{2,1,0:T(8,128)(2,1)}, u32[]{:S(2)}, u32[]{:S(2)}) collective-permute-start(bf16[16,128,128]{2,1,0:T(8,128)(2,1)} %get-tuple-element.33), channel_id=1, source_target_pairs={{0,4},{4,0},{1,5},{5,1},{2,6},{6,2},{3,7},{7,3},{8,12},{12,8},{9,1... | collective-permute-start | bytes 1572872 | tf_op jit(solution)/shard_map/ppermute | solution.py:527
  37.2 39.7 %collective-permute-start.8 = (bf16[8,128,256]{2,1,0:T(8,128)(2,1)}, bf16[8,128,256]{2,1,0:T(8,128)(2,1)}, u32[]{:S(2)}, u32[]{:S(2)}) collective-permute-start(bf16[8,128,256]{2,1,0:T(8,128)(2,1)} %bitcast.11), channel_id=1, source_target_pairs={{0,2},{1,3},{2,0},{3,1},{4,6},{5,7},{6,4},{7,5},{8,10},{9,11},{10,... | collective-permute-start | bytes 1572872 | tf_op jit(solution)/shard_map/ppermute | solution.py:492
  38.4 39.2 %collective-permute-start.7 = (bf16[8,128,256]{2,1,0:T(8,128)(2,1)}, bf16[8,128,256]{2,1,0:T(8,128)(2,1)}, u32[]{:S(2)}, u32[]{:S(2)}) collective-permute-start(bf16[8,128,256]{2,1,0:T(8,128)(2,1)} %collective-permute-done.refs_1_), channel_id=1, source_target_pairs={{0,1},{1,2},{2,3},{3,0},{4,5},{5,6},{6,7},{7,4},{8,9},{9,10},{10,1... | collective-permute-start | bytes 1572872 | tf_op jit(solution)/shard_map/ppermute | solution.py:492
  70.4 10.8 %collective-permute-start.3 = (bf16[8,128,128]{2,1,0:T(8,128)(2,1)S(1)}, bf16[8,128,128]{2,1,0:T(8,128)(2,1)S(1)}, u32[]{:S(2)}, u32[]{:S(2)}) collective-permute-start(bf16[8,128,128]{2,1,0:T(8,128)(2,1)S(1)} %get-tuple-element.35), channel_id=1, source_target_pairs={{0,8},{8,16},{16,24},{24,0},{1,9},{9,17},{17,25},{25,1},{2,10},{10... | collective-permute-start | bytes 786440 | tf_op jit(solution)/shard_map/ppermute | solution.py:509
  73.2 10.1 %collective-permute-start.4 = (bf16[8,128,128]{2,1,0:T(8,128)(2,1)S(1)}, bf16[8,128,128]{2,1,0:T(8,128)(2,1)S(1)}, u32[]{:S(2)}, u32[]{:S(2)}) collective-permute-start(bf16[8,128,128]{2,1,0:T(8,128)(2,1)S(1)} %get-tuple-element.36), channel_id=1, source_target_pairs={{0,16},{8,24},{16,0},{24,8},{1,17},{9,25},{17,1},{25,9},{2,18},{10... | collective-permute-start | bytes 786440 | tf_op jit(solution)/shard_map/ppermute | solution.py:509
  76.9 10.3 %collective-permute-start.5 = (bf16[8,128,128]{2,1,0:T(8,128)(2,1)S(1)}, bf16[8,128,128]{2,1,0:T(8,128)(2,1)S(1)}, u32[]{:S(2)}, u32[]{:S(2)}) collective-permute-start(bf16[8,128,128]{2,1,0:T(8,128)(2,1)S(1)} %get-tuple-element.37), channel_id=1, source_target_pairs={{0,24},{8,0},{16,8},{24,16},{1,25},{9,1},{17,9},{25,17},{2,26},{10... | collective-permute-start | bytes 786440 | tf_op jit(solution)/shard_map/ppermute | solution.py:509
  90.8 3.5 %collective-permute-start.9 = (f32[16,128,128]{2,1,0:T(8,128)S(1)}, f32[16,128,128]{2,1,0:T(8,128)S(1)}, u32[]{:S(2)}, u32[]{:S(2)}) collective-permute-start(f32[16,128,128]{2,1,0:T(8,128)S(1)} %get-tuple-element.40.refs_3_), channel_id=1, source_target_pairs={{0,4},{4,0},{1,5},{5,1},{2,6},{6,2},{3,7},{7,3},{8,12},{12,8},{9,1... | collective-permute-start | bytes 3145736 | tf_op jit(solution)/shard_map/ppermute | solution.py:547
  90.9 3.4 %collective-permute-start.10 = (f32[8,128,128]{2,1,0:T(8,128)S(1)}, f32[8,128,128]{2,1,0:T(8,128)S(1)}, u32[]{:S(2)}, u32[]{:S(2)}) collective-permute-start(f32[8,128,128]{2,1,0:T(8,128)S(1)} %get-tuple-element.41.refs_4_), channel_id=1, source_target_pairs={{0,4},{4,0},{1,5},{5,1},{2,6},{6,2},{3,7},{7,3},{8,12},{12,8},{9,1... | collective-permute-start | bytes 1572872 | tf_op jit(solution)/shard_map/ppermute | solution.py:548
  96.8 58.1 %copy-start.2 = (f32[1,128,512]{2,1,0:T(8,128)S(1)}, f32[1,128,512]{2,1,0:T(8,128)}, u32[]{:S(2)}) copy-start(f32[1,128,512]{2,1,0:T(8,128)} %param.9) | copy-start | bytes 786436
  96.8 22.4 %collective-permute-start.11 = (bf16[8,128,256]{2,1,0:T(8,128)(2,1)S(1)}, bf16[8,128,256]{2,1,0:T(8,128)(2,1)S(1)}, u32[]{:S(2)}, u32[]{:S(2)}) collective-permute-start(bf16[8,128,256]{2,1,0:T(8,128)(2,1)S(1)} %get-tuple-element.45), channel_id=1, source_target_pairs={{0,8},{8,16},{16,24},{24,0},{1,9},{9,17},{17,25},{25,1},{2,10},{10... | collective-permute-start | bytes 1572872 | tf_op jit(solution)/shard_map/ppermute | solution.py:509
  96.9 22.3 %collective-permute-start.12 = (bf16[8,128,256]{2,1,0:T(8,128)(2,1)S(1)}, bf16[8,128,256]{2,1,0:T(8,128)(2,1)S(1)}, u32[]{:S(2)}, u32[]{:S(2)}) collective-permute-start(bf16[8,128,256]{2,1,0:T(8,128)(2,1)S(1)} %get-tuple-element.46), channel_id=1, source_target_pairs={{0,16},{8,24},{16,0},{24,8},{1,17},{9,25},{17,1},{25,9},{2,18},{10... | collective-permute-start | bytes 1572872 | tf_op jit(solution)/shard_map/ppermute | solution.py:509
  97.1 26.6 %collective-permute-start.13 = (bf16[8,128,256]{2,1,0:T(8,128)(2,1)S(1)}, bf16[8,128,256]{2,1,0:T(8,128)(2,1)S(1)}, u32[]{:S(2)}, u32[]{:S(2)}) collective-permute-start(bf16[8,128,256]{2,1,0:T(8,128)(2,1)S(1)} %get-tuple-element.47), channel_id=1, source_target_pairs={{0,24},{8,0},{16,8},{24,16},{1,25},{9,1},{17,9},{25,17},{2,26},{10... | collective-permute-start | bytes 1572872 | tf_op jit(solution)/shard_map/ppermute | solution.py:509
  148.9 4.3 %collective-permute-start.14 = (f32[128,128]{1,0:T(8,128)S(1)}, f32[128,128]{1,0:T(8,128)S(1)}, u32[]{:S(2)}, u32[]{:S(2)}) collective-permute-start(f32[128,128]{1,0:T(8,128)S(1)} %get-tuple-element.50.refs_4_), channel_id=1, source_target_pairs={{0,1},{1,2},{2,3},{3,0},{4,5},{5,6},{6,7},{7,4},{8,9},{9,10},{10,1... | collective-permute-start | bytes 196616 | tf_op jit(solution)/shard_map/ppermute | solution.py:492
  149.0 5.9 %collective-permute-start.15 = (f32[128,128]{1,0:T(8,128)S(1)}, f32[128,128]{1,0:T(8,128)S(1)}, u32[]{:S(2)}, u32[]{:S(2)}) collective-permute-start(f32[128,128]{1,0:T(8,128)S(1)} %get-tuple-element.51.refs_5_), channel_id=1, source_target_pairs={{0,2},{1,3},{2,0},{3,1},{4,6},{5,7},{6,4},{7,5},{8,10},{9,11},{10,... | collective-permute-start | bytes 196616 | tf_op jit(solution)/shard_map/ppermute | solution.py:492
where the time goes:
time: 158 us; the launch traced here: 156 us
  blocking collectives  63.2 us (40%)
  Pallas kernels  47.2 us (30%)
  waiting for transfers between devices  28 us (18%)
  starting transfers between devices  14.9 us (9%)
  local copies, waits for them, and re-layouts  1.76 us (1%)
    all_to_all x2, blocking collectives, sum_y(): return (own, lax.all_to_all(sends, 'z', 0, 0, tiled=True))  41.3 us
    pallas_call x3, Pallas kernels, grid_call(): pl.pallas_call(kernel, grid=(1,), in_specs=in_specs, out_specs=[spec for...  30.9 us
    psum x1, blocking collectives, on_device(): known = lax.psum(known, COL)  21.9 us
    pallas_call x8, Pallas kernels, call(): pl.pallas_call(body, in_specs=specs + [ANY_SPEC] * n_more, out_specs=[pl....  16.3 us
    ppermute x6, waiting for transfers between devices, along_y(): return [lax.ppermute(s, 'y', ring(ny, d + 1)) for d, s in enumerate(sends)]  14.1 us
    ppermute x7, waiting for transfers between devices, send(): return lax.ppermute(blocks, 'row', ring(4, distance))  10.9 us
    ppermute x7, starting transfers between devices, send(): return lax.ppermute(blocks, 'row', ring(4, distance))  8.46 us
    ppermute x6, starting transfers between devices, along_y(): return [lax.ppermute(s, 'y', ring(ny, d + 1)) for d, s in enumerate(sends)]  5.81 us
  transfers between devices with their start and end apart: 16, of which 10 were waited for; matrix products, arithmetic and copies ran while one was open for 0% of the time, Pallas kernels for 15%

commit v1 on v0

--- a/solution.py
+++ b/solution.py
@@ -321,29 +321,31 @@
             lax.fori_loop(0, half, step_across, 0, unroll=4)
 
 
-def pack(block):
+def places():
     lane = lax.broadcasted_iota(jnp.int32, (BLK, BLK), 1)
     row = lax.broadcasted_iota(jnp.int32, (BLK, BLK), 0)
-    first = block
-    hi = first.astype(BF16).astype(F32)
-    rest = jnp.sum(jnp.where(lane == row, first - hi, 0.0), axis=1, keepdims=True)
-    first = jnp.where(lane > row, 0.0, first)
-    first = jnp.where(lane == row + 1, rest, first)
-    last = jnp.sum(jnp.where((lane == row) & (row == BLK - 1), block - hi, 0.0), keepdims=True)
-    first = jnp.where((row == 0) & (lane == BLK - 1), last, first)
-    return first.astype(BF16)
+    return lane, row
+
+
+def pack(block):
+    lane, row = places()
+    rest = jnp.where(lane == row, block - block.astype(BF16).astype(F32), 0.0)
+    moved = pltpu.roll(rest, BLK - 1, 0)
+    first = pltpu.roll(rest[:8], BLK - 1, 1)
+    upper = jnp.where(lane == row + 1, moved, 0.0)
+    top = jnp.where((row[:8] == 0) & (lane[:8] == BLK - 1), first, upper[:8])
+    upper = jnp.concatenate([top, upper[8:]], axis=0)
+    return jnp.where(lane > row, upper, block).astype(BF16)
 
 
 def unpack(block):
-    lane = lax.broadcasted_iota(jnp.int32, (BLK, BLK), 1)
-    row = lax.broadcasted_iota(jnp.int32, (BLK, BLK), 0)
-    first = block.astype(F32)
-    last = jnp.sum(jnp.where((row == 0) & (lane == BLK - 1), first, 0.0), keepdims=True)
-    rest = jnp.sum(jnp.where(lane == row + 1, first, 0.0), axis=1, keepdims=True)
-    rest = jnp.where((row == BLK - 1), last, rest)
-    first = jnp.where(lane == row, first + rest, first)
-    first = jnp.where(lane > row, 0.0, first)
-    return first
+    lane, row = places()
+    block = block.astype(F32)
+    moved = pltpu.roll(block, 1, 0)
+    first = pltpu.roll(block[:8], 1, 1)
+    top = jnp.where(row[:8] == 0, first, moved[:8])
+    rest = jnp.concatenate([top, moved[8:]], axis=0)
+    return jnp.where(lane > row, 0.0, jnp.where(lane == row, block + rest, block))
 
 
 def known_kernel(info_ref, id_ref, names_ref, out_ref):
@@ -523,7 +525,8 @@
     solved, rounded, part, diag, packed = second_chunk(at_row, w, own[0], panel, solved, hop)
     own.append(blocks(rounded))
     right.append(send(own[1], -1))
-    across = [send(hop, 1), send(blocks(part), 2)]
+    across = [send(hop, 1)]
+    hop = send(blocks(part), 1)
     their_diag = lax.ppermute(packed, "core", ring(2, 1))
 
     (known,) = call(
@@ -535,6 +538,8 @@
         deps=[diag, right[0]],
     )
     known = lax.psum(known, COL)
+    (hop,) = call(lambda info: None, [info], [], name="pass_on", deps=[known], through=[hop])
+    across.append(send(hop, 1))
     own_diag, *sends = after_scatter(scatter_diag_kernel, [diag, their_diag], BLK, "scatter_diag")
     got_diag = along_y(sends)
     off_right, off_across = call(
@@ -542,7 +547,7 @@
         [at_row, *own, *right, *across],
         [f32_out(count, BLK, BLK), f32_out(half, BLK, BLK)],
         name="products",
-        deps=got_diag,
+        deps=[got_diag[0], got_diag[2]],
     )
     their_right = lax.ppermute(off_right, "core", ring(2, 1))
     their_across = lax.ppermute(off_across, "core", ring(2, 1))

time: 158 us -> 149 us (0.943)
  blocking collectives: 63.2 us -> 57.1 us
  Pallas kernels: 47.2 us -> 45.6 us
    all_to_all x2, blocking collectives: 41.3 us -> 35.2 us  [sum_y(): return (own, lax.all_to_all(sends, 'z', 0, 0, tiled=True))]
    ppermute x7 -> x8, waiting for transfers between devices: 10.9 us -> 8.54 us  [send(): return lax.ppermute(blocks, 'row', ring(4, distance))]
    ppermute x6, waiting for transfers between devices: 14.1 us -> 16.1 us  [along_y(): return [lax.ppermute(s, 'y', ring(ny, d + 1)) for d, s in enumerate(sends)]]
    ppermute x7 -> x8, starting transfers between devices: 8.46 us -> 9.85 us  [send(): return lax.ppermute(blocks, 'row', ring(4, distance))]
    pallas_call x8 -> x9, Pallas kernels: 16.3 us -> 15.1 us  [call(): pl.pallas_call(body, in_specs=specs + [ANY_SPEC] * n_more, out_specs=[pl....]
  transfers between devices with their start and end apart: 16 -> 17, of which waited for: 10 -> 9; matrix products, arithmetic and copies ran while one was open for 0% -> 0% of each run, Pallas kernels for 15% -> 17%
where the time goes in v1:
time: 149 us; the launch traced here: 148 us
  blocking collectives  57.1 us (38%)
  Pallas kernels  45.6 us (31%)
  waiting for transfers between devices  27.6 us (19%)
  starting transfers between devices  14.9 us (10%)
  local copies, waits for them, and re-layouts  1.77 us (1%)
    all_to_all x2, blocking collectives, sum_y(): return (own, lax.all_to_all(sends, 'z', 0, 0, tiled=True))  35.2 us
    pallas_call x3, Pallas kernels, grid_call(): pl.pallas_call(kernel, grid=(1,), in_specs=in_specs, out_specs=[spec for...  30.5 us
    psum x1, blocking collectives, on_device(): known = lax.psum(known, COL)  21.9 us
    ppermute x6, waiting for transfers between devices, along_y(): return [lax.ppermute(s, 'y', ring(ny, d + 1)) for d, s in enumerate(sends)]  16.1 us
    pallas_call x9, Pallas kernels, call(): pl.pallas_call(body, in_specs=specs + [ANY_SPEC] * n_more, out_specs=[pl....  15.1 us
    ppermute x8, starting transfers between devices, send(): return lax.ppermute(blocks, 'row', ring(4, distance))  9.85 us
    ppermute x8, waiting for transfers between devices, send(): return lax.ppermute(blocks, 'row', ring(4, distance))  8.54 us
    ppermute x6, starting transfers between devices, along_y(): return [lax.ppermute(s, 'y', ring(ny, d + 1)) for d, s in enumerate(sends)]  4.51 us
  transfers between devices with their start and end apart: 17, of which 9 were waited for; matrix products, arithmetic and copies ran while one was open for 0% of the time, Pallas kernels for 17%

profile of v1, /device:TPU:26, one launch (start us, length us, event | category | flops | bytes accessed | tf_op | source)
XLA Modules:
  0.0 148.4 jit_solution(2580584404042879748)
XLA Ops:
  0.6 1.6 %copy-done.1 = f32[2,512,512]{2,1,0:T(8,128)S(1)} copy-done((f32[2,512,512]{2,1,0:T(8,128)S(1)}, f32[2,512,512]{2,1,0:T(8,128)}, u32[]{:S(2)}) %copy-start.1) | copy-done | bytes 2097176
  2.2 14.0 %first_chunk.1 = (f32[2,256,512]{2,1,0:T(8,128)S(1)}, f32[2,1024,512]{2,1,0:T(8,128)}, bf16[2,1024,256]{2,1,0:T(8,128)(2,1)S(1)}, bf16[1024,256]{1,0:T(8,128)(2,1)S(1)}) custom-call(s32[1]{0:T(128)} %bitcast.info_ref.refs_0_, f32[2,512,512]{2,1,0:T(8,128)S(1)} %copy-done.1, f32[2,1024,512]{2,1,0:T(8,128)} %bitcast.13), custom_call_target="tpu_custom_call" | custom-call | flops 1000000 | bytes 10000 | tf_op jit(solution)/shard_map/first_chunk/pallas_call | solution.py:206
  16.2 0.6 collective-permute-start.1
  16.8 1.5 %collective-permute-start = (bf16[8,128,256]{2,1,0:T(8,128)(2,1)S(1)}, bf16[8,128,256]{2,1,0:T(8,128)(2,1)S(1)}, u32[]{:S(2)}, u32[]{:S(2)}) collective-permute-start(bf16[8,128,256]{2,1,0:T(8,128)(2,1)S(1)} %bitcast.19), channel_id=1, source_target_pairs={{0,1},{1,2},{2,3},{3,0},{4,5},{5,6},{6,7},{7,4},{8,9},{9,10},{10,1... | collective-permute-start | bytes 1572872 | tf_op jit(solution)/shard_map/ppermute | solution.py:494
  18.3 11.5 %second_factor.1.w_ref = f32[2,256,512]{2,1,0:T(8,128)S(1)} custom-call(f32[2,512,512]{2,1,0:T(8,128)S(1)} %copy-done.1, f32[2,256,512]{2,1,0:T(8,128)S(1)} %get-tuple-element.27.refs_0_), custom_call_target="tpu_custom_call" | custom-call | flops 1000000 | bytes 10000 | tf_op jit(solution)/shard_map/second_factor/pallas_call | solution.py:206
  29.9 1.3 collective-permute-done.refs_1_
  31.2 4.9 %second_chunk.1 = (f32[2,1024,512]{2,1,0:T(8,128)}, bf16[2,1024,256]{2,1,0:T(8,128)(2,1)}, bf16[1024,256]{1,0:T(8,128)(2,1)}, f32[16,128,128]{2,1,0:T(8,128)S(1)}, bf16[16,128,128]{2,1,0:T(8,128)(2,1)}) custom-call(s32[1]{0:T(128)} %bitcast.info_ref.refs_0_, f32[2,256,512]{2,1,0:T(8,128)S(1)} %second_factor.1.w_ref, ...), custom_call_target="tpu_custom_call", output_to_operand_aliasing={{0}: (4, {})} | custom-call | flops 1000000 | bytes 10000 | tf_op jit(solution)/shard_map/second_chunk/pallas_call | solution.py:206
  36.2 0.5 collective-permute-start.8
  36.7 2.7 %collective-permute-start.6 = (bf16[16,128,256]{2,1,0:T(8,128)(2,1)}, bf16[16,128,256]{2,1,0:T(8,128)(2,1)}, u32[]{:S(2)}, u32[]{:S(2)}) collective-permute-start(bf16[16,128,256]{2,1,0:T(8,128)(2,1)} %bitcast.10.refs_2_), channel_id=1, source_target_pairs={{0,3},{1,0},{2,1},{3,2},{4,7},{5,4},{6,5},{7,6},{8,11},{9,8},{10,9... | collective-permute-start | bytes 3145736 | tf_op jit(solution)/shard_map/ppermute | solution.py:494
  39.4 0.0 collective-permute-start.2
  39.4 0.1 reshape.36.refs_2_
  40.1 0.1 stack.20.refs_0_
  40.2 0.0 collective-permute-start.7
  40.2 2.1 %collective-permute-done.1.refs_4_.refs_3_ = bf16[16,128,256]{2,1,0:T(8,128)(2,1)S(1)} collective-permute-done((bf16[16,128,256]{2,1,0:T(8,128)(2,1)S(1)}, bf16[16,128,256]{2,1,0:T(8,128)(2,1)S(1)}, u32[]{:S(2)}, u32[]{:S(2)}) %collective-permute-start.1) | collective-permute-done | bytes 1048608 | tf_op jit(solution)/shard_map/ppermute | solution.py:494
  42.4 0.6 known.1
  42.9 21.9 %psum.7.refs_1_ = s32[9,128]{1,0:T(8,128)S(1)} all-reduce(s32[9,128]{1,0:T(8,128)S(1)} %known.1), channel_id=1, replica_groups=mesh['z'=8,'y'=4,'core'=2,'row'=4] {'z','y','core'}, use_global_device_ids=true, to_apply=%region_0.0 | all-reduce | flops 1152 | bytes 9216 | tf_op jit(solution)/shard_map/psum | solution.py:540
  64.8 0.0 collective-permute-done.8.refs_2_
  64.9 0.5 pass_on.1
  65.4 1.6 %collective-permute-start.9 = (bf16[8,128,256]{2,1,0:T(8,128)(2,1)}, bf16[8,128,256]{2,1,0:T(8,128)(2,1)S(1)}, u32[]{:S(2)}, u32[]{:S(2)}) collective-permute-start(bf16[8,128,256]{2,1,0:T(8,128)(2,1)} %pass_on.1), channel_id=1, source_target_pairs={{0,1},{1,2},{2,3},{3,0},{4,5},{5,6},{6,7},{7,4},{8,9},{9,10},{10,1... | collective-permute-start | bytes 1572872 | tf_op jit(solution)/shard_map/ppermute | solution.py:494
  67.0 3.3 %scatter_diag.1 = (f32[8,128,128]{2,1,0:T(8,128)S(1)}, bf16[8,128,128]{2,1,0:T(8,128)(2,1)S(1)}, bf16[8,128,128]{2,1,0:T(8,128)(2,1)S(1)}, bf16[8,128,128]{2,1,0:T(8,128)(2,1)S(1)}) custom-call(s32[5]{0:T(128)S(1)} %stack.20.refs_0_, s32[9,128]{1,0:T(8,128)S(1)} %psum.7.refs_1_, s32[16]{0:T(128)S(1)} %reshape.36.refs_2_, ...), custom_call_target="tpu_custom_call" | custom-call | flops 1000000 | bytes 10000 | tf_op jit(solution)/shard_map/scatter_diag/pallas_call | solution.py:286
  70.2 2.4 %collective-permute-start.3 = (bf16[8,128,128]{2,1,0:T(8,128)(2,1)S(1)}, bf16[8,128,128]{2,1,0:T(8,128)(2,1)S(1)}, u32[]{:S(2)}, u32[]{:S(2)}) collective-permute-start(bf16[8,128,128]{2,1,0:T(8,128)(2,1)S(1)} %get-tuple-element.35), channel_id=1, source_target_pairs={{0,8},{8,16},{16,24},{24,0},{1,9},{9,17},{17,25},{25,1},{2,10},{10... | collective-permute-start | bytes 786440 | tf_op jit(solution)/shard_map/ppermute | solution.py:511
  72.6 4.0 %collective-permute-done.3.refs_7_.refs_2_ = bf16[8,128,128]{2,1,0:T(8,128)(2,1)S(1)} collective-permute-done((bf16[8,128,128]{2,1,0:T(8,128)(2,1)S(1)}, bf16[8,128,128]{2,1,0:T(8,128)(2,1)S(1)}, u32[]{:S(2)}, u32[]{:S(2)}) %collective-permute-start.3) | collective-permute-done | bytes 262176 | tf_op jit(solution)/shard_map/ppermute | solution.py:511
  76.7 3.5 %collective-permute-done.5.refs_8_.refs_4_ = bf16[8,128,128]{2,1,0:T(8,128)(2,1)S(1)} collective-permute-done((bf16[8,128,128]{2,1,0:T(8,128)(2,1)S(1)}, bf16[8,128,128]{2,1,0:T(8,128)(2,1)S(1)}, u32[]{:S(2)}, u32[]{:S(2)}) %collective-permute-start.5) | collective-permute-done | bytes 262176 | tf_op jit(solution)/shard_map/ppermute | solution.py:511
  80.2 3.5 %products.1 = (f32[16,128,128]{2,1,0:T(8,128)S(1)}, f32[8,128,128]{2,1,0:T(8,128)S(1)}) custom-call(s32[1]{0:T(128)} %bitcast.info_ref.refs_0_, bf16[16,128,256]{2,1,0:T(8,128)(2,1)S(1)} %bitcast.17, bf16[16,128,256]{2,1,0:T(8,128)(2,1)} %bitcast.10.refs_2_, bf16[16,128,256]{2,1,0:T(8,128)(2,1)S(1)} %collective-permute-done.1.refs_4_.refs_3_, ...), custom_call_target="tpu_custom_call" | custom-call | flops 1000000 | bytes 10000 | tf_op jit(solution)/shard_map/products/pallas_call | solution.py:286
  83.7 0.1 collective-permute-start.10
  83.8 0.5 collective-permute-start.11
  84.3 0.0 collective-permute-start.4
  84.3 2.9 %collective-permute-done.11.refs_6_ = f32[8,128,128]{2,1,0:T(8,128)S(1)} collective-permute-done((f32[8,128,128]{2,1,0:T(8,128)S(1)}, f32[8,128,128]{2,1,0:T(8,128)S(1)}, u32[]{:S(2)}, u32[]{:S(2)}) %collective-permute-start.11) | collective-permute-done | bytes 524320 | tf_op jit(solution)/shard_map/ppermute | solution.py:553
  87.2 0.0 collective-permute-done.10.refs_5_
  87.2 2.5 %scatter_off.1 = (f32[8,128,256]{2,1,0:T(8,128)S(1)}, bf16[8,128,256]{2,1,0:T(8,128)(2,1)S(1)}, bf16[8,128,256]{2,1,0:T(8,128)(2,1)S(1)}, bf16[8,128,256]{2,1,0:T(8,128)(2,1)S(1)}) custom-call(s32[5]{0:T(128)S(1)} %stack.20.refs_0_, s32[9,128]{1,0:T(8,128)S(1)} %psum.7.refs_1_, s32[16]{0:T(128)S(1)} %reshape.36.refs_2_, ...), custom_call_target="tpu_custom_call" | custom-call | flops 1000000 | bytes 10000 | tf_op jit(solution)/shard_map/scatter_off/pallas_call | solution.py:286
  89.7 0.0 copy-start.3
  89.7 0.1 collective-permute-start.12
  89.8 0.8 collective-permute-start.13
  90.6 1.2 collective-permute-start.14
  91.8 2.3 %collective-permute-done.4.refs_3_ = bf16[8,128,128]{2,1,0:T(8,128)(2,1)S(1)} collective-permute-done((bf16[8,128,128]{2,1,0:T(8,128)(2,1)S(1)}, bf16[8,128,128]{2,1,0:T(8,128)(2,1)S(1)}, u32[]{:S(2)}, u32[]{:S(2)}) %collective-permute-start.4) | collective-permute-done | bytes 262176 | tf_op jit(solution)/shard_map/ppermute | solution.py:511
  94.1 1.8 %sum_diag.1 = (f32[128,128]{1,0:T(8,128)S(1)}, bf16[8,128,128]{2,1,0:T(8,128)(2,1)S(1)}) custom-call(s32[5]{0:T(128)S(1)} %stack.20.refs_0_, f32[8,128,128]{2,1,0:T(8,128)S(1)} %get-tuple-element.34.refs_1_, bf16[8,128,128]{2,1,0:T(8,128)(2,1)S(1)} %collective-permute-done.3.refs_7_.refs_2_, bf16[8,128,128]{2,1,0:T(8,128)(2,1)S(1)} %collective-permute-done.4.refs_3_, ...), custom_call_target="tpu_custom_call" | custom-call | flops 1000000 | bytes 10000 | tf_op jit(solution)/shard_map/sum_diag/pallas_call | solution.py:286
  95.9 14.4 %all_to_all.10.refs_5_.refs_3_ = bf16[8,128,128]{2,1,0:T(8,128)(2,1)S(1)} all-to-all(bf16[8,128,128]{2,1,0:T(8,128)(2,1)S(1)} %get-tuple-element.44), channel_id=1, replica_groups=mesh['z'=8,'y'=4,'core'=2,'row'=4] {'z'}, dimensions={0} | all-to-all | bytes 524288 | tf_op jit(solution)/shard_map/all_to_all | solution.py:518
  110.3 0.0 collective-permute-done.12.refs_2_
  110.3 0.0 collective-permute-done.13.refs_3_
  110.3 6.3 %collective-permute-done.14.refs_4_ = bf16[8,128,256]{2,1,0:T(8,128)(2,1)S(1)} collective-permute-done((bf16[8,128,256]{2,1,0:T(8,128)(2,1)S(1)}, bf16[8,128,256]{2,1,0:T(8,128)(2,1)S(1)}, u32[]{:S(2)}, u32[]{:S(2)}) %collective-permute-start.14) | collective-permute-done | bytes 524320 | tf_op jit(solution)/shard_map/ppermute | solution.py:511
  116.6 0.8 sum_off.1
  117.4 20.8 %all_to_all.11.refs_2_ = bf16[8,128,256]{2,1,0:T(8,128)(2,1)S(1)} all-to-all(bf16[8,128,256]{2,1,0:T(8,128)(2,1)S(1)} %get-tuple-element.49), channel_id=1, replica_groups=mesh['z'=8,'y'=4,'core'=2,'row'=4] {'z'}, dimensions={0} | all-to-all | bytes 1048576 | tf_op jit(solution)/shard_map/all_to_all | solution.py:518
  138.2 0.7 last_sum.1
  138.9 2.3 %collective-permute-start.15 = (f32[128,128]{1,0:T(8,128)S(1)}, f32[128,128]{1,0:T(8,128)S(1)}, u32[]{:S(2)}, u32[]{:S(2)}) collective-permute-start(f32[128,128]{1,0:T(8,128)S(1)} %get-tuple-element.50.refs_4_), channel_id=1, source_target_pairs={{0,1},{1,2},{2,3},{3,0},{4,5},{5,6},{6,7},{7,4},{8,9},{9,10},{10,1... | collective-permute-start | bytes 196616 | tf_op jit(solution)/shard_map/ppermute | solution.py:494
  141.2 0.7 collective-permute-start.16
  141.9 1.8 %collective-permute-done.15.refs_6_ = f32[128,128]{1,0:T(8,128)S(1)} collective-permute-done((f32[128,128]{1,0:T(8,128)S(1)}, f32[128,128]{1,0:T(8,128)S(1)}, u32[]{:S(2)}, u32[]{:S(2)}) %collective-permute-start.15) | collective-permute-done | bytes 65568 | tf_op jit(solution)/shard_map/ppermute | solution.py:494
  143.7 3.2 %collective-permute-done.16.refs_7_ = f32[128,128]{1,0:T(8,128)S(1)} collective-permute-done((f32[128,128]{1,0:T(8,128)S(1)}, f32[128,128]{1,0:T(8,128)S(1)}, u32[]{:S(2)}, u32[]{:S(2)}) %collective-permute-start.16) | collective-permute-done | bytes 65568 | tf_op jit(solution)/shard_map/ppermute | solution.py:494
  146.9 1.5 %finish.1 = f32[128,512]{1,0:T(8,128)} custom-call(s32[5]{0:T(128)S(1)} %stack.20.refs_0_, f32[128,512]{1,0:T(8,128)S(1)} %bitcast.18, f32[128,128]{1,0:T(8,128)S(1)} %get-tuple-element.43.refs_2_, bf16[8,128,128]{2,1,0:T(8,128)(2,1)S(1)} %all_to_all.10.refs_5_.refs_3_, f32[128,128]{1,0:T(8,128)S(1)} %get-tuple-element.50.refs_4_, ...), custom_call_target="tpu_custom_call" | custom-call | flops 1000000 | bytes 10000 | tf_op jit(solution)/shard_map/finish/pallas_call | solution.py:286
  (13 shorter events, 0.0 us)
Async XLA Ops:
  0.6 1.6 %copy-start.1 = (f32[2,512,512]{2,1,0:T(8,128)S(1)}, f32[2,512,512]{2,1,0:T(8,128)}, u32[]{:S(2)}) copy-start(f32[2,512,512]{2,1,0:T(8,128)} %diag_ref.3) | copy-start | bytes 6291460
  2.2 29.0 %copy-start = (f32[2,8,128,512]{3,2,1,0:T(8,128)S(1)}, f32[2,8,128,512]{3,2,1,0:T(8,128)}, u32[]{:S(2)}) copy-start(f32[2,8,128,512]{3,2,1,0:T(8,128)} %param.6) | copy-start | bytes 12582916
  16.2 26.1 %collective-permute-start.1 = (bf16[16,128,256]{2,1,0:T(8,128)(2,1)S(1)}, bf16[16,128,256]{2,1,0:T(8,128)(2,1)S(1)}, u32[]{:S(2)}, u32[]{:S(2)}) collective-permute-start(bf16[16,128,256]{2,1,0:T(8,128)(2,1)S(1)} %bitcast.15), channel_id=1, source_target_pairs={{0,3},{1,0},{2,1},{3,2},{4,7},{5,4},{6,5},{7,6},{8,11},{9,8},{10,9... | collective-permute-start | bytes 3145736 | tf_op jit(solution)/shard_map/ppermute | solution.py:494
  16.8 14.4 %collective-permute-start = (bf16[8,128,256]{2,1,0:T(8,128)(2,1)S(1)}, bf16[8,128,256]{2,1,0:T(8,128)(2,1)S(1)}, u32[]{:S(2)}, u32[]{:S(2)}) collective-permute-start(bf16[8,128,256]{2,1,0:T(8,128)(2,1)S(1)} %bitcast.19), channel_id=1, source_target_pairs={{0,1},{1,2},{2,3},{3,0},{4,5},{5,6},{6,7},{7,4},{8,9},{9,10},{10,1... | collective-permute-start | bytes 1572872 | tf_op jit(solution)/shard_map/ppermute | solution.py:494
  31.2 4.9 %copy-start.2 = (bf16[8,128,256]{2,1,0:T(8,128)(2,1)}, bf16[8,128,256]{2,1,0:T(8,128)(2,1)S(1)}, u32[]{:S(2)}) copy-start(bf16[8,128,256]{2,1,0:T(8,128)(2,1)S(1)} %collective-permute-done.refs_1_) | copy-start | bytes 1572868
  31.2 8.1 %copy-start.4 = (s32[2,8]{1,0:T(2,128)S(1)}, s32[2,8]{1,0:T(2,128)}, u32[]{:S(2)}) copy-start(s32[2,8]{1,0:T(2,128)} %param.7) | copy-start | bytes 196
  36.2 28.7 %collective-permute-start.8 = (bf16[8,128,256]{2,1,0:T(8,128)(2,1)}, bf16[8,128,256]{2,1,0:T(8,128)(2,1)}, u32[]{:S(2)}, u32[]{:S(2)}) collective-permute-start(bf16[8,128,256]{2,1,0:T(8,128)(2,1)} %bitcast.11), channel_id=1, source_target_pairs={{0,1},{1,2},{2,3},{3,0},{4,5},{5,6},{6,7},{7,4},{8,9},{9,10},{10,1... | collective-permute-start | bytes 1572872 | tf_op jit(solution)/shard_map/ppermute | solution.py:494
  36.7 43.5 %collective-permute-start.6 = (bf16[16,128,256]{2,1,0:T(8,128)(2,1)}, bf16[16,128,256]{2,1,0:T(8,128)(2,1)}, u32[]{:S(2)}, u32[]{:S(2)}) collective-permute-start(bf16[16,128,256]{2,1,0:T(8,128)(2,1)} %bitcast.10.refs_2_), channel_id=1, source_target_pairs={{0,3},{1,0},{2,1},{3,2},{4,7},{5,4},{6,5},{7,6},{8,11},{9,8},{10,9... | collective-permute-start | bytes 3145736 | tf_op jit(solution)/shard_map/ppermute | solution.py:494
  39.4 27.6 %collective-permute-start.2 = (bf16[16,128,128]{2,1,0:T(8,128)(2,1)}, bf16[16,128,128]{2,1,0:T(8,128)(2,1)}, u32[]{:S(2)}, u32[]{:S(2)}) collective-permute-start(bf16[16,128,128]{2,1,0:T(8,128)(2,1)} %get-tuple-element.33), channel_id=1, source_target_pairs={{0,4},{4,0},{1,5},{5,1},{2,6},{6,2},{3,7},{7,3},{8,12},{12,8},{9,1... | collective-permute-start | bytes 1572872 | tf_op jit(solution)/shard_map/ppermute | solution.py:530
  40.2 32.4 %collective-permute-start.7 = (bf16[8,128,256]{2,1,0:T(8,128)(2,1)}, bf16[8,128,256]{2,1,0:T(8,128)(2,1)}, u32[]{:S(2)}, u32[]{:S(2)}) collective-permute-start(bf16[8,128,256]{2,1,0:T(8,128)(2,1)} %copy-done.2), channel_id=1, source_target_pairs={{0,1},{1,2},{2,3},{3,0},{4,5},{5,6},{6,7},{7,4},{8,9},{9,10},{10,1... | collective-permute-start | bytes 1572872 | tf_op jit(solution)/shard_map/ppermute | solution.py:494
  65.4 14.8 %collective-permute-start.9 = (bf16[8,128,256]{2,1,0:T(8,128)(2,1)}, bf16[8,128,256]{2,1,0:T(8,128)(2,1)S(1)}, u32[]{:S(2)}, u32[]{:S(2)}) collective-permute-start(bf16[8,128,256]{2,1,0:T(8,128)(2,1)} %pass_on.1), channel_id=1, source_target_pairs={{0,1},{1,2},{2,3},{3,0},{4,5},{5,6},{6,7},{7,4},{8,9},{9,10},{10,1... | collective-permute-start | bytes 1572872 | tf_op jit(solution)/shard_map/ppermute | solution.py:494
  70.2 6.4 %collective-permute-start.3 = (bf16[8,128,128]{2,1,0:T(8,128)(2,1)S(1)}, bf16[8,128,128]{2,1,0:T(8,128)(2,1)S(1)}, u32[]{:S(2)}, u32[]{:S(2)}) collective-permute-start(bf16[8,128,128]{2,1,0:T(8,128)(2,1)S(1)} %get-tuple-element.35), channel_id=1, source_target_pairs={{0,8},{8,16},{16,24},{24,0},{1,9},{9,17},{17,25},{25,1},{2,10},{10... | collective-permute-start | bytes 786440 | tf_op jit(solution)/shard_map/ppermute | solution.py:511
  72.6 7.6 %collective-permute-start.5 = (bf16[8,128,128]{2,1,0:T(8,128)(2,1)S(1)}, bf16[8,128,128]{2,1,0:T(8,128)(2,1)S(1)}, u32[]{:S(2)}, u32[]{:S(2)}) collective-permute-start(bf16[8,128,128]{2,1,0:T(8,128)(2,1)S(1)} %get-tuple-element.37), channel_id=1, source_target_pairs={{0,24},{8,0},{16,8},{24,16},{1,25},{9,1},{17,9},{25,17},{2,26},{10... | collective-permute-start | bytes 786440 | tf_op jit(solution)/shard_map/ppermute | solution.py:511
  83.7 3.5 %collective-permute-start.10 = (f32[16,128,128]{2,1,0:T(8,128)S(1)}, f32[16,128,128]{2,1,0:T(8,128)S(1)}, u32[]{:S(2)}, u32[]{:S(2)}) collective-permute-start(f32[16,128,128]{2,1,0:T(8,128)S(1)} %get-tuple-element.40.refs_3_), channel_id=1, source_target_pairs={{0,4},{4,0},{1,5},{5,1},{2,6},{6,2},{3,7},{7,3},{8,12},{12,8},{9,1... | collective-permute-start | bytes 3145736 | tf_op jit(solution)/shard_map/ppermute | solution.py:552
  83.8 3.4 %collective-permute-start.11 = (f32[8,128,128]{2,1,0:T(8,128)S(1)}, f32[8,128,128]{2,1,0:T(8,128)S(1)}, u32[]{:S(2)}, u32[]{:S(2)}) collective-permute-start(f32[8,128,128]{2,1,0:T(8,128)S(1)} %get-tuple-element.41.refs_4_), channel_id=1, source_target_pairs={{0,4},{4,0},{1,5},{5,1},{2,6},{6,2},{3,7},{7,3},{8,12},{12,8},{9,1... | collective-permute-start | bytes 1572872 | tf_op jit(solution)/shard_map/ppermute | solution.py:553
  84.3 9.8 %collective-permute-start.4 = (bf16[8,128,128]{2,1,0:T(8,128)(2,1)S(1)}, bf16[8,128,128]{2,1,0:T(8,128)(2,1)S(1)}, u32[]{:S(2)}, u32[]{:S(2)}) collective-permute-start(bf16[8,128,128]{2,1,0:T(8,128)(2,1)S(1)} %get-tuple-element.36), channel_id=1, source_target_pairs={{0,16},{8,24},{16,0},{24,8},{1,17},{9,25},{17,1},{25,9},{2,18},{10... | collective-permute-start | bytes 786440 | tf_op jit(solution)/shard_map/ppermute | solution.py:511
  89.7 57.2 %copy-start.3 = (f32[1,128,512]{2,1,0:T(8,128)S(1)}, f32[1,128,512]{2,1,0:T(8,128)}, u32[]{:S(2)}) copy-start(f32[1,128,512]{2,1,0:T(8,128)} %param.9) | copy-start | bytes 786436
  89.7 20.6 %collective-permute-start.12 = (bf16[8,128,256]{2,1,0:T(8,128)(2,1)S(1)}, bf16[8,128,256]{2,1,0:T(8,128)(2,1)S(1)}, u32[]{:S(2)}, u32[]{:S(2)}) collective-permute-start(bf16[8,128,256]{2,1,0:T(8,128)(2,1)S(1)} %get-tuple-element.45), channel_id=1, source_target_pairs={{0,8},{8,16},{16,24},{24,0},{1,9},{9,17},{17,25},{25,1},{2,10},{10... | collective-permute-start | bytes 1572872 | tf_op jit(solution)/shard_map/ppermute | solution.py:511
  89.8 20.5 %collective-permute-start.13 = (bf16[8,128,256]{2,1,0:T(8,128)(2,1)S(1)}, bf16[8,128,256]{2,1,0:T(8,128)(2,1)S(1)}, u32[]{:S(2)}, u32[]{:S(2)}) collective-permute-start(bf16[8,128,256]{2,1,0:T(8,128)(2,1)S(1)} %get-tuple-element.46), channel_id=1, source_target_pairs={{0,16},{8,24},{16,0},{24,8},{1,17},{9,25},{17,1},{25,9},{2,18},{10... | collective-permute-start | bytes 1572872 | tf_op jit(solution)/shard_map/ppermute | solution.py:511
  90.6 26.0 %collective-permute-start.14 = (bf16[8,128,256]{2,1,0:T(8,128)(2,1)S(1)}, bf16[8,128,256]{2,1,0:T(8,128)(2,1)S(1)}, u32[]{:S(2)}, u32[]{:S(2)}) collective-permute-start(bf16[8,128,256]{2,1,0:T(8,128)(2,1)S(1)} %get-tuple-element.47), channel_id=1, source_target_pairs={{0,24},{8,0},{16,8},{24,16},{1,25},{9,1},{17,9},{25,17},{2,26},{10... | collective-permute-start | bytes 1572872 | tf_op jit(solution)/shard_map/ppermute | solution.py:511
  138.9 4.8 %collective-permute-start.15 = (f32[128,128]{1,0:T(8,128)S(1)}, f32[128,128]{1,0:T(8,128)S(1)}, u32[]{:S(2)}, u32[]{:S(2)}) collective-permute-start(f32[128,128]{1,0:T(8,128)S(1)} %get-tuple-element.50.refs_4_), channel_id=1, source_target_pairs={{0,1},{1,2},{2,3},{3,0},{4,5},{5,6},{6,7},{7,4},{8,9},{9,10},{10,1... | collective-permute-start | bytes 196616 | tf_op jit(solution)/shard_map/ppermute | solution.py:494
  141.2 5.8 %collective-permute-start.16 = (f32[128,128]{1,0:T(8,128)S(1)}, f32[128,128]{1,0:T(8,128)S(1)}, u32[]{:S(2)}, u32[]{:S(2)}) collective-permute-start(f32[128,128]{1,0:T(8,128)S(1)} %get-tuple-element.51.refs_5_), channel_id=1, source_target_pairs={{0,2},{1,3},{2,0},{3,1},{4,6},{5,7},{6,4},{7,5},{8,10},{9,11},{10,... | collective-permute-start | bytes 196616 | tf_op jit(solution)/shard_map/ppermute | solution.py:494

commit v2 on v1

--- a/solution.py
+++ b/solution.py
@@ -180,8 +180,10 @@
     solve_part(0, FIRST, sn, info_ref, w_ref, b_ref, x_ref, r_refs, half_ref)
 
 
-def second_kernel(sn, info_ref, w_ref, own_ref, b_ref, *refs):
-    x_ref, r_ref, half_ref, product_ref, packed_ref = refs[2:]
+def second_kernel(sn, info_ref, w_ref, own_ref, b_ref, hop_ref, _, x_ref, r_ref, both_ref, product_ref, packed_ref):
+    for c in range(hop_ref.shape[0]):
+        both_ref[BLK * c : BLK * (c + 1), :FIRST] = hop_ref[c]
+    half_ref = both_ref.at[:, pl.ds(FIRST, FIRST)]
     r_refs = [r_ref.at[s] for s in range(sn)]
     solve_part(FIRST, b_ref.shape[2], sn, info_ref, w_ref, b_ref, x_ref, r_refs, half_ref)
     anc = b_ref.shape[1] // BLK
@@ -252,24 +254,24 @@
     )[0]
 
 
-def second_chunk(row, w, own, panel, solved, dep):
+def second_chunk(row, w, own, panel, hop, solved):
     sn, rows, width = panel.shape
     count = own.shape[0]
     return grid_call(
         functools.partial(second_kernel, sn),
-        [row, w, own, panel, solved, dep],
-        [SMEM_SPEC, whole(w.shape), whole(own.shape), whole(panel.shape), ANY_SPEC, ANY_SPEC],
+        [row, w, own, panel, hop, solved],
+        [SMEM_SPEC, whole(w.shape), whole(own.shape), whole(panel.shape), whole(hop.shape), ANY_SPEC],
         [
             (pl.BlockSpec((sn, rows, FIRST), lambda i: (0, 0, 1)), f32_out(sn, rows, width)),
             (whole((sn, rows, FIRST)), bf16_out(sn, rows, FIRST)),
-            (whole((rows, FIRST)), bf16_out(rows, FIRST)),
+            (whole((rows, width)), bf16_out(rows, width)),
             (whole((count, BLK, BLK)), f32_out(count, BLK, BLK)),
             (whole((count, BLK, BLK)), bf16_out(count, BLK, BLK)),
         ],
         "second_chunk",
         [],
         VMEM_LIMIT,
-        {4: 0},
+        {5: 0},
     )
 
 
@@ -297,7 +299,8 @@
 
 
 def products_kernel(n, info_ref, *refs):
-    own, right, across, (right_ref, across_ref) = refs[:n], refs[n : 2 * n], refs[2 * n : -2], refs[-2:]
+    own, right, (near_ref, far_ref, *outs) = refs[:n], refs[n : 2 * n], refs[2 * n :]
+    right_ref, across_ref, right_send, across_send = outs
     half = across_ref.shape[0]
     nt = ((1,), (1,))
     for s in range(2):
@@ -306,12 +309,16 @@
             return jnp.concatenate([r[s * half + c] for r in group], axis=1)
 
         def step(c, carry):
-            right_ref[s * half + c] = dot_dims(joined(own, c), joined(right, c), nt)
+            product = dot_dims(joined(own, c), joined(right, c), nt)
+            right_ref[s * half + c] = product
+            right_send[s * half + c] = product.astype(BF16)
             return carry
 
         def step_across(c, carry):
-            other = jnp.concatenate([r[c] for r in across], axis=1)
-            across_ref[c] = dot_dims(joined(own, c), other, nt)
+            other = jnp.concatenate([near_ref[c, :, :FIRST], far_ref[c]], axis=1)
+            product = dot_dims(joined(own, c), other, nt)
+            across_ref[c] = product
+            across_send[c] = product.astype(BF16)
             return carry
 
         lax.fori_loop(0, half, step, 0, unroll=4)
@@ -346,6 +353,10 @@
     top = jnp.where(row[:8] == 0, first, moved[:8])
     rest = jnp.concatenate([top, moved[8:]], axis=0)
     return jnp.where(lane > row, 0.0, jnp.where(lane == row, block + rest, block))
+
+
+def pass_on_kernel(hop_ref, part_ref):
+    part_ref[...] = hop_ref[:, :, FIRST:]
 
 
 def known_kernel(info_ref, id_ref, names_ref, out_ref):
@@ -370,7 +381,7 @@
         @pl.when(lax.rem(p, 2) == core)
         def _():
             at = lax.div(p, 2)
-            acc[at, :, lanes] += widen(ref[c])
+            acc[at, :, lanes] += widen(ref[c]).astype(F32)
 
         return carry
 
@@ -522,10 +533,9 @@
     right = [send(own[0], -1)]
     hop = send(blocks(part), 1)
     w = second_factor(diag_blocks, w)
-    solved, rounded, part, diag, packed = second_chunk(at_row, w, own[0], panel, solved, hop)
+    solved, rounded, part, diag, packed = second_chunk(at_row, w, own[0], panel, hop, solved)
     own.append(blocks(rounded))
     right.append(send(own[1], -1))
-    across = [send(hop, 1)]
     hop = send(blocks(part), 1)
     their_diag = lax.ppermute(packed, "core", ring(2, 1))
 
@@ -538,19 +548,19 @@
         deps=[diag, right[0]],
     )
     known = lax.psum(known, COL)
-    (hop,) = call(lambda info: None, [info], [], name="pass_on", deps=[known], through=[hop])
-    across.append(send(hop, 1))
+    (part,) = call(pass_on_kernel, [hop], [bf16_out(half, rows, FIRST)], name="pass_on", smem=0, deps=[known])
+    across = [hop, send(part, 1)]
     own_diag, *sends = after_scatter(scatter_diag_kernel, [diag, their_diag], BLK, "scatter_diag")
     got_diag = along_y(sends)
-    off_right, off_across = call(
+    off_right, off_across, send_right, send_across = call(
         functools.partial(products_kernel, len(own)),
         [at_row, *own, *right, *across],
-        [f32_out(count, BLK, BLK), f32_out(half, BLK, BLK)],
+        [out(n, BLK, BLK) for out in (f32_out, bf16_out) for n in (count, half)],
         name="products",
         deps=[got_diag[0], got_diag[2]],
     )
-    their_right = lax.ppermute(off_right, "core", ring(2, 1))
-    their_across = lax.ppermute(off_across, "core", ring(2, 1))
+    their_right = lax.ppermute(send_right, "core", ring(2, 1))
+    their_across = lax.ppermute(send_across, "core", ring(2, 1))
     own_off, *sends = after_scatter(
         scatter_off_kernel, [off_right, off_across, their_right, their_across], 2 * BLK, "scatter_off"
     )

time: 149 us -> 150 us (level)
  blocking collectives: 57.1 us -> 55.6 us
    pallas_call x3, Pallas kernels: 30.5 us -> 32.4 us  [grid_call(): pl.pallas_call(kernel, grid=(1,), in_specs=in_specs, out_specs=[spec for...]
    all_to_all x2, blocking collectives: 35.2 us -> 33.7 us  [sum_y(): return (own, lax.all_to_all(sends, 'z', 0, 0, tiled=True))]
    ppermute x8 -> x7, starting transfers between devices: 9.85 us -> 9.15 us  [send(): return lax.ppermute(blocks, 'row', ring(4, distance))]
    ppermute x8 -> x7, waiting for transfers between devices: 8.54 us -> 8.71 us  [send(): return lax.ppermute(blocks, 'row', ring(4, distance))]
  transfers between devices with their start and end apart: 17 -> 16, of which waited for: 9 -> 9; matrix products, arithmetic and copies ran while one was open for 0% -> 0% of each run, Pallas kernels for 17% -> 17%
where the time goes in v2:
time: 150 us; the launch traced here: 149 us
  blocking collectives  55.6 us (37%)
  Pallas kernels  47 us (31%)
  waiting for transfers between devices  27.9 us (19%)
  starting transfers between devices  15.7 us (10%)
  local copies, waits for them, and re-layouts  1.76 us (1%)
    all_to_all x2, blocking collectives, sum_y(): return (own, lax.all_to_all(sends, 'z', 0, 0, tiled=True))  33.7 us
    pallas_call x3, Pallas kernels, grid_call(): pl.pallas_call(kernel, grid=(1,), in_specs=in_specs, out_specs=[spec for...  32.4 us
    psum x1, blocking collectives, on_device(): known = lax.psum(known, COL)  21.9 us
    ppermute x6, waiting for transfers between devices, along_y(): return [lax.ppermute(s, 'y', ring(ny, d + 1)) for d, s in enumerate(sends)]  17.4 us
    pallas_call x9, Pallas kernels, call(): pl.pallas_call(body, in_specs=specs + [ANY_SPEC] * n_more, out_specs=[pl....  14.6 us
    ppermute x7, starting transfers between devices, send(): return lax.ppermute(blocks, 'row', ring(4, distance))  9.15 us
    ppermute x7, waiting for transfers between devices, send(): return lax.ppermute(blocks, 'row', ring(4, distance))  8.71 us
    ppermute x6, starting transfers between devices, along_y(): return [lax.ppermute(s, 'y', ring(ny, d + 1)) for d, s in enumerate(sends)]  5.99 us
  transfers between devices with their start and end apart: 16, of which 9 were waited for; matrix products, arithmetic and copies ran while one was open for 0% of the time, Pallas kernels for 17%

profile of v2, /device:TPU:26, one launch (start us, length us, event | category | flops | bytes accessed | tf_op | source)
XLA Modules:
  0.0 149.4 jit_solution(8076388084861166496)
XLA Ops:
  0.6 1.6 %copy-done.1 = f32[2,512,512]{2,1,0:T(8,128)S(1)} copy-done((f32[2,512,512]{2,1,0:T(8,128)S(1)}, f32[2,512,512]{2,1,0:T(8,128)}, u32[]{:S(2)}) %copy-start.1) | copy-done | bytes 2097176
  2.2 14.4 %first_chunk.1 = (f32[2,256,512]{2,1,0:T(8,128)S(1)}, f32[2,1024,512]{2,1,0:T(8,128)}, bf16[2,1024,256]{2,1,0:T(8,128)(2,1)}, bf16[1024,256]{1,0:T(8,128)(2,1)S(1)}) custom-call(s32[1]{0:T(128)} %bitcast.info_ref.refs_0_, f32[2,512,512]{2,1,0:T(8,128)S(1)} %copy-done.1, f32[2,1024,512]{2,1,0:T(8,128)} %bitcast.13), custom_call_target="tpu_custom_call" | custom-call | flops 1000000 | bytes 10000 | tf_op jit(solution)/shard_map/first_chunk/pallas_call | solution.py:208
  16.7 1.6 %collective-permute-start = (bf16[8,128,256]{2,1,0:T(8,128)(2,1)S(1)}, bf16[8,128,256]{2,1,0:T(8,128)(2,1)S(1)}, u32[]{:S(2)}, u32[]{:S(2)}) collective-permute-start(bf16[8,128,256]{2,1,0:T(8,128)(2,1)S(1)} %bitcast.16), channel_id=1, source_target_pairs={{0,1},{1,2},{2,3},{3,0},{4,5},{5,6},{6,7},{7,4},{8,9},{9,10},{10,1... | collective-permute-start | bytes 1572872 | tf_op jit(solution)/shard_map/ppermute | solution.py:505
  18.2 0.5 collective-permute-start.1
  18.8 11.6 %second_factor.1.w_ref = f32[2,256,512]{2,1,0:T(8,128)S(1)} custom-call(f32[2,512,512]{2,1,0:T(8,128)S(1)} %copy-done.1, f32[2,256,512]{2,1,0:T(8,128)S(1)} %get-tuple-element.29.refs_0_), custom_call_target="tpu_custom_call" | custom-call | flops 1000000 | bytes 10000 | tf_op jit(solution)/shard_map/second_factor/pallas_call | solution.py:208
  30.4 0.1 collective-permute-done.hop_ref
  30.4 6.4 %second_chunk.1 = (f32[2,1024,512]{2,1,0:T(8,128)}, bf16[2,1024,256]{2,1,0:T(8,128)(2,1)}, bf16[1024,512]{1,0:T(8,128)(2,1)}, f32[16,128,128]{2,1,0:T(8,128)S(1)}, bf16[16,128,128]{2,1,0:T(8,128)(2,1)}) custom-call(s32[1]{0:T(128)} %bitcast.info_ref.refs_0_, f32[2,256,512]{2,1,0:T(8,128)S(1)} %second_factor.1.w_ref, ...), custom_call_target="tpu_custom_call", output_to_operand_aliasing={{0}: (5, {})} | custom-call | flops 1000000 | bytes 10000 | tf_op jit(solution)/shard_map/second_chunk/pallas_call | solution.py:208
  36.8 1.5 %collective-permute-start.7 = (bf16[8,128,512]{2,1,0:T(8,128)(2,1)}, bf16[8,128,512]{2,1,0:T(8,128)(2,1)S(1)}, u32[]{:S(2)}, u32[]{:S(2)}) collective-permute-start(bf16[8,128,512]{2,1,0:T(8,128)(2,1)} %bitcast.11), channel_id=1, source_target_pairs={{0,1},{1,2},{2,3},{3,0},{4,5},{5,6},{6,7},{7,4},{8,9},{9,10},{10,1... | collective-permute-start | bytes 3145736 | tf_op jit(solution)/shard_map/ppermute | solution.py:505
  38.3 0.5 collective-permute-start.6
  38.9 0.0 collective-permute-start.2
  38.9 0.1 reshape.36.refs_2_
  39.6 0.1 stack.20.refs_0_
  39.7 4.8 %collective-permute-done.1.refs_4_.refs_3_ = bf16[16,128,256]{2,1,0:T(8,128)(2,1)S(1)} collective-permute-done((bf16[16,128,256]{2,1,0:T(8,128)(2,1)}, bf16[16,128,256]{2,1,0:T(8,128)(2,1)S(1)}, u32[]{:S(2)}, u32[]{:S(2)}) %collective-permute-start.1) | collective-permute-done | bytes 1048608 | tf_op jit(solution)/shard_map/ppermute | solution.py:505
  44.5 0.6 known.1
  45.1 21.9 %psum.7.refs_1_ = s32[9,128]{1,0:T(8,128)S(1)} all-reduce(s32[9,128]{1,0:T(8,128)S(1)} %known.1), channel_id=1, replica_groups=mesh['z'=8,'y'=4,'core'=2,'row'=4] {'z','y','core'}, use_global_device_ids=true, to_apply=%region_0.0 | all-reduce | flops 1152 | bytes 9216 | tf_op jit(solution)/shard_map/psum | solution.py:550
  67.0 0.0 collective-permute-done.7.refs_0_.refs_5_
  67.1 1.3 collective-permute-start.8
  68.4 3.1 %scatter_diag.1 = (f32[8,128,128]{2,1,0:T(8,128)S(1)}, bf16[8,128,128]{2,1,0:T(8,128)(2,1)S(1)}, bf16[8,128,128]{2,1,0:T(8,128)(2,1)S(1)}, bf16[8,128,128]{2,1,0:T(8,128)(2,1)S(1)}) custom-call(s32[5]{0:T(128)S(1)} %stack.20.refs_0_, s32[9,128]{1,0:T(8,128)S(1)} %psum.7.refs_1_, s32[16]{0:T(128)S(1)} %reshape.36.refs_2_, ...), custom_call_target="tpu_custom_call" | custom-call | flops 1000000 | bytes 10000 | tf_op jit(solution)/shard_map/scatter_diag/pallas_call | solution.py:288
  71.4 2.8 %collective-permute-start.3 = (bf16[8,128,128]{2,1,0:T(8,128)(2,1)S(1)}, bf16[8,128,128]{2,1,0:T(8,128)(2,1)S(1)}, u32[]{:S(2)}, u32[]{:S(2)}) collective-permute-start(bf16[8,128,128]{2,1,0:T(8,128)(2,1)S(1)} %get-tuple-element.37), channel_id=1, source_target_pairs={{0,8},{8,16},{16,24},{24,0},{1,9},{9,17},{17,25},{25,1},{2,10},{10... | collective-permute-start | bytes 786440 | tf_op jit(solution)/shard_map/ppermute | solution.py:522
  74.2 0.0 collective-permute-start.5
  74.2 3.9 %collective-permute-done.3.refs_7_.refs_2_ = bf16[8,128,128]{2,1,0:T(8,128)(2,1)S(1)} collective-permute-done((bf16[8,128,128]{2,1,0:T(8,128)(2,1)S(1)}, bf16[8,128,128]{2,1,0:T(8,128)(2,1)S(1)}, u32[]{:S(2)}, u32[]{:S(2)}) %collective-permute-start.3) | collective-permute-done | bytes 262176 | tf_op jit(solution)/shard_map/ppermute | solution.py:522
  78.1 3.7 %collective-permute-done.5.refs_8_.refs_4_ = bf16[8,128,128]{2,1,0:T(8,128)(2,1)S(1)} collective-permute-done((bf16[8,128,128]{2,1,0:T(8,128)(2,1)S(1)}, bf16[8,128,128]{2,1,0:T(8,128)(2,1)S(1)}, u32[]{:S(2)}, u32[]{:S(2)}) %collective-permute-start.5) | collective-permute-done | bytes 262176 | tf_op jit(solution)/shard_map/ppermute | solution.py:522
  81.8 0.0 collective-permute-done.6.refs_4_
  81.8 3.7 %products.1 = (f32[16,128,128]{2,1,0:T(8,128)S(1)}, f32[8,128,128]{2,1,0:T(8,128)S(1)}, bf16[16,128,128]{2,1,0:T(8,128)(2,1)S(1)}, bf16[8,128,128]{2,1,0:T(8,128)(2,1)S(1)}) custom-call(s32[1]{0:T(128)} %bitcast.info_ref.refs_0_, bf16[16,128,256]{2,1,0:T(8,128)(2,1)} %bitcast.2.own_ref.refs_1_, bf16[16,128,256]{2,1,0:T(8,128)(2,1)} %bitcast.10.refs_2_, ...), custom_call_target="tpu_custom_call" | custom-call | flops 1000000 | bytes 10000 | tf_op jit(solution)/shard_map/products/pallas_call | solution.py:288
  85.5 0.1 collective-permute-start.9
  85.6 0.5 collective-permute-start.10
  86.1 0.0 collective-permute-start.4
  86.1 1.8 %collective-permute-done.10.refs_6_ = bf16[8,128,128]{2,1,0:T(8,128)(2,1)S(1)} collective-permute-done((bf16[8,128,128]{2,1,0:T(8,128)(2,1)S(1)}, bf16[8,128,128]{2,1,0:T(8,128)(2,1)S(1)}, u32[]{:S(2)}, u32[]{:S(2)}) %collective-permute-start.10) | collective-permute-done | bytes 262176 | tf_op jit(solution)/shard_map/ppermute | solution.py:563
  87.9 0.0 collective-permute-done.9.refs_5_
  87.9 2.5 %scatter_off.1 = (f32[8,128,256]{2,1,0:T(8,128)S(1)}, bf16[8,128,256]{2,1,0:T(8,128)(2,1)S(1)}, bf16[8,128,256]{2,1,0:T(8,128)(2,1)S(1)}, bf16[8,128,256]{2,1,0:T(8,128)(2,1)S(1)}) custom-call(s32[5]{0:T(128)S(1)} %stack.20.refs_0_, s32[9,128]{1,0:T(8,128)S(1)} %psum.7.refs_1_, s32[16]{0:T(128)S(1)} %reshape.36.refs_2_, ...), custom_call_target="tpu_custom_call" | custom-call | flops 1000000 | bytes 10000 | tf_op jit(solution)/shard_map/scatter_off/pallas_call | solution.py:288
  90.4 0.0 copy-start.2
  90.4 0.1 collective-permute-start.11
  90.5 1.8 %collective-permute-start.12 = (bf16[8,128,256]{2,1,0:T(8,128)(2,1)S(1)}, bf16[8,128,256]{2,1,0:T(8,128)(2,1)S(1)}, u32[]{:S(2)}, u32[]{:S(2)}) collective-permute-start(bf16[8,128,256]{2,1,0:T(8,128)(2,1)S(1)} %get-tuple-element.50), channel_id=1, source_target_pairs={{0,16},{8,24},{16,0},{24,8},{1,17},{9,25},{17,1},{25,9},{2,18},{10... | collective-permute-start | bytes 1572872 | tf_op jit(solution)/shard_map/ppermute | solution.py:522
  92.2 1.3 collective-permute-start.13
  93.5 3.3 %collective-permute-done.4.refs_3_ = bf16[8,128,128]{2,1,0:T(8,128)(2,1)S(1)} collective-permute-done((bf16[8,128,128]{2,1,0:T(8,128)(2,1)S(1)}, bf16[8,128,128]{2,1,0:T(8,128)(2,1)S(1)}, u32[]{:S(2)}, u32[]{:S(2)}) %collective-permute-start.4) | collective-permute-done | bytes 262176 | tf_op jit(solution)/shard_map/ppermute | solution.py:522
  96.9 1.8 %sum_diag.1 = (f32[128,128]{1,0:T(8,128)S(1)}, bf16[8,128,128]{2,1,0:T(8,128)(2,1)S(1)}) custom-call(s32[5]{0:T(128)S(1)} %stack.20.refs_0_, f32[8,128,128]{2,1,0:T(8,128)S(1)} %get-tuple-element.36.refs_1_, bf16[8,128,128]{2,1,0:T(8,128)(2,1)S(1)} %collective-permute-done.3.refs_7_.refs_2_, bf16[8,128,128]{2,1,0:T(8,128)(2,1)S(1)} %collective-permute-done.4.refs_3_, ...), custom_call_target="tpu_custom_call" | custom-call | flops 1000000 | bytes 10000 | tf_op jit(solution)/shard_map/sum_diag/pallas_call | solution.py:288
  98.7 13.2 %all_to_all.10.refs_5_.refs_3_ = bf16[8,128,128]{2,1,0:T(8,128)(2,1)S(1)} all-to-all(bf16[8,128,128]{2,1,0:T(8,128)(2,1)S(1)} %get-tuple-element.48), channel_id=1, replica_groups=mesh['z'=8,'y'=4,'core'=2,'row'=4] {'z'}, dimensions={0} | all-to-all | bytes 524288 | tf_op jit(solution)/shard_map/all_to_all | solution.py:529
  111.9 0.0 collective-permute-done.11.refs_2_
  111.9 0.0 collective-permute-done.12.refs_3_
  111.9 6.5 %collective-permute-done.13.refs_4_ = bf16[8,128,256]{2,1,0:T(8,128)(2,1)S(1)} collective-permute-done((bf16[8,128,256]{2,1,0:T(8,128)(2,1)S(1)}, bf16[8,128,256]{2,1,0:T(8,128)(2,1)S(1)}, u32[]{:S(2)}, u32[]{:S(2)}) %collective-permute-start.13) | collective-permute-done | bytes 524320 | tf_op jit(solution)/shard_map/ppermute | solution.py:522
  118.4 0.8 sum_off.1
  119.2 20.4 %all_to_all.11.refs_2_ = bf16[8,128,256]{2,1,0:T(8,128)(2,1)S(1)} all-to-all(bf16[8,128,256]{2,1,0:T(8,128)(2,1)S(1)} %get-tuple-element.53), channel_id=1, replica_groups=mesh['z'=8,'y'=4,'core'=2,'row'=4] {'z'}, dimensions={0} | all-to-all | bytes 1048576 | tf_op jit(solution)/shard_map/all_to_all | solution.py:529
  139.7 0.7 last_sum.1
  140.3 1.8 %collective-permute-start.14 = (f32[128,128]{1,0:T(8,128)S(1)}, f32[128,128]{1,0:T(8,128)S(1)}, u32[]{:S(2)}, u32[]{:S(2)}) collective-permute-start(f32[128,128]{1,0:T(8,128)S(1)} %get-tuple-element.54.refs_4_), channel_id=1, source_target_pairs={{0,1},{1,2},{2,3},{3,0},{4,5},{5,6},{6,7},{7,4},{8,9},{9,10},{10,1... | collective-permute-start | bytes 196616 | tf_op jit(solution)/shard_map/ppermute | solution.py:505
  142.1 2.0 %collective-permute-start.15 = (f32[128,128]{1,0:T(8,128)S(1)}, f32[128,128]{1,0:T(8,128)S(1)}, u32[]{:S(2)}, u32[]{:S(2)}) collective-permute-start(f32[128,128]{1,0:T(8,128)S(1)} %get-tuple-element.55.refs_5_), channel_id=1, source_target_pairs={{0,2},{1,3},{2,0},{3,1},{4,6},{5,7},{6,4},{7,5},{8,10},{9,11},{10,... | collective-permute-start | bytes 196616 | tf_op jit(solution)/shard_map/ppermute | solution.py:505
  144.1 0.6 collective-permute-done.14.refs_6_
  144.7 3.2 %collective-permute-done.15.refs_7_ = f32[128,128]{1,0:T(8,128)S(1)} collective-permute-done((f32[128,128]{1,0:T(8,128)S(1)}, f32[128,128]{1,0:T(8,128)S(1)}, u32[]{:S(2)}, u32[]{:S(2)}) %collective-permute-start.15) | collective-permute-done | bytes 65568 | tf_op jit(solution)/shard_map/ppermute | solution.py:505
  147.9 1.5 %finish.1 = f32[128,512]{1,0:T(8,128)} custom-call(s32[5]{0:T(128)S(1)} %stack.20.refs_0_, f32[128,512]{1,0:T(8,128)S(1)} %bitcast.15, f32[128,128]{1,0:T(8,128)S(1)} %get-tuple-element.47.refs_2_, bf16[8,128,128]{2,1,0:T(8,128)(2,1)S(1)} %all_to_all.10.refs_5_.refs_3_, f32[128,128]{1,0:T(8,128)S(1)} %get-tuple-element.54.refs_4_, ...), custom_call_target="tpu_custom_call" | custom-call | flops 1000000 | bytes 10000 | tf_op jit(solution)/shard_map/finish/pallas_call | solution.py:288
  (9 shorter events, 0.1 us)
Async XLA Ops:
  0.6 1.6 %copy-start.1 = (f32[2,512,512]{2,1,0:T(8,128)S(1)}, f32[2,512,512]{2,1,0:T(8,128)}, u32[]{:S(2)}) copy-start(f32[2,512,512]{2,1,0:T(8,128)} %diag_ref.3) | copy-start | bytes 6291460
  2.2 28.2 %copy-start = (f32[2,8,128,512]{3,2,1,0:T(8,128)S(1)}, f32[2,8,128,512]{3,2,1,0:T(8,128)}, u32[]{:S(2)}) copy-start(f32[2,8,128,512]{3,2,1,0:T(8,128)} %param.6) | copy-start | bytes 12582916
  16.7 13.7 %collective-permute-start = (bf16[8,128,256]{2,1,0:T(8,128)(2,1)S(1)}, bf16[8,128,256]{2,1,0:T(8,128)(2,1)S(1)}, u32[]{:S(2)}, u32[]{:S(2)}) collective-permute-start(bf16[8,128,256]{2,1,0:T(8,128)(2,1)S(1)} %bitcast.16), channel_id=1, source_target_pairs={{0,1},{1,2},{2,3},{3,0},{4,5},{5,6},{6,7},{7,4},{8,9},{9,10},{10,1... | collective-permute-start | bytes 1572872 | tf_op jit(solution)/shard_map/ppermute | solution.py:505
  18.2 26.3 %collective-permute-start.1 = (bf16[16,128,256]{2,1,0:T(8,128)(2,1)}, bf16[16,128,256]{2,1,0:T(8,128)(2,1)S(1)}, u32[]{:S(2)}, u32[]{:S(2)}) collective-permute-start(bf16[16,128,256]{2,1,0:T(8,128)(2,1)} %bitcast.2.own_ref.refs_1_), channel_id=1, source_target_pairs={{0,3},{1,0},{2,1},{3,2},{4,7},{5,4},{6,5},{7,6},{8,11},{9,8},{10,9... | collective-permute-start | bytes 3145736 | tf_op jit(solution)/shard_map/ppermute | solution.py:505
  30.4 8.4 %copy-start.3 = (s32[2,8]{1,0:T(2,128)S(1)}, s32[2,8]{1,0:T(2,128)}, u32[]{:S(2)}) copy-start(s32[2,8]{1,0:T(2,128)} %param.7) | copy-start | bytes 196
  36.8 30.2 %collective-permute-start.7 = (bf16[8,128,512]{2,1,0:T(8,128)(2,1)}, bf16[8,128,512]{2,1,0:T(8,128)(2,1)S(1)}, u32[]{:S(2)}, u32[]{:S(2)}) collective-permute-start(bf16[8,128,512]{2,1,0:T(8,128)(2,1)} %bitcast.11), channel_id=1, source_target_pairs={{0,1},{1,2},{2,3},{3,0},{4,5},{5,6},{6,7},{7,4},{8,9},{9,10},{10,1... | collective-permute-start | bytes 3145736 | tf_op jit(solution)/shard_map/ppermute | solution.py:505
  38.3 43.5 %collective-permute-start.6 = (bf16[16,128,256]{2,1,0:T(8,128)(2,1)}, bf16[16,128,256]{2,1,0:T(8,128)(2,1)}, u32[]{:S(2)}, u32[]{:S(2)}) collective-permute-start(bf16[16,128,256]{2,1,0:T(8,128)(2,1)} %bitcast.10.refs_2_), channel_id=1, source_target_pairs={{0,3},{1,0},{2,1},{3,2},{4,7},{5,4},{6,5},{7,6},{8,11},{9,8},{10,9... | collective-permute-start | bytes 3145736 | tf_op jit(solution)/shard_map/ppermute | solution.py:505
  38.9 29.5 %collective-permute-start.2 = (bf16[16,128,128]{2,1,0:T(8,128)(2,1)}, bf16[16,128,128]{2,1,0:T(8,128)(2,1)}, u32[]{:S(2)}, u32[]{:S(2)}) collective-permute-start(bf16[16,128,128]{2,1,0:T(8,128)(2,1)} %get-tuple-element.35), channel_id=1, source_target_pairs={{0,4},{4,0},{1,5},{5,1},{2,6},{6,2},{3,7},{7,3},{8,12},{12,8},{9,1... | collective-permute-start | bytes 1572872 | tf_op jit(solution)/shard_map/ppermute | solution.py:540
  67.1 14.8 %collective-permute-start.8 = (bf16[8,128,256]{2,1,0:T(8,128)(2,1)S(1)}, bf16[8,128,256]{2,1,0:T(8,128)(2,1)S(1)}, u32[]{:S(2)}, u32[]{:S(2)}) collective-permute-start(bf16[8,128,256]{2,1,0:T(8,128)(2,1)S(1)} %pass_on.1), channel_id=1, source_target_pairs={{0,1},{1,2},{2,3},{3,0},{4,5},{5,6},{6,7},{7,4},{8,9},{9,10},{10,1... | collective-permute-start | bytes 1572872 | tf_op jit(solution)/shard_map/ppermute | solution.py:505
  71.4 6.7 %collective-permute-start.3 = (bf16[8,128,128]{2,1,0:T(8,128)(2,1)S(1)}, bf16[8,128,128]{2,1,0:T(8,128)(2,1)S(1)}, u32[]{:S(2)}, u32[]{:S(2)}) collective-permute-start(bf16[8,128,128]{2,1,0:T(8,128)(2,1)S(1)} %get-tuple-element.37), channel_id=1, source_target_pairs={{0,8},{8,16},{16,24},{24,0},{1,9},{9,17},{17,25},{25,1},{2,10},{10... | collective-permute-start | bytes 786440 | tf_op jit(solution)/shard_map/ppermute | solution.py:522
  74.2 7.6 %collective-permute-start.5 = (bf16[8,128,128]{2,1,0:T(8,128)(2,1)S(1)}, bf16[8,128,128]{2,1,0:T(8,128)(2,1)S(1)}, u32[]{:S(2)}, u32[]{:S(2)}) collective-permute-start(bf16[8,128,128]{2,1,0:T(8,128)(2,1)S(1)} %get-tuple-element.39), channel_id=1, source_target_pairs={{0,24},{8,0},{16,8},{24,16},{1,25},{9,1},{17,9},{25,17},{2,26},{10... | collective-permute-start | bytes 786440 | tf_op jit(solution)/shard_map/ppermute | solution.py:522
  85.5 2.4 %collective-permute-start.9 = (bf16[16,128,128]{2,1,0:T(8,128)(2,1)S(1)}, bf16[16,128,128]{2,1,0:T(8,128)(2,1)S(1)}, u32[]{:S(2)}, u32[]{:S(2)}) collective-permute-start(bf16[16,128,128]{2,1,0:T(8,128)(2,1)S(1)} %get-tuple-element.44), channel_id=1, source_target_pairs={{0,4},{4,0},{1,5},{5,1},{2,6},{6,2},{3,7},{7,3},{8,12},{12,8},{9,1... | collective-permute-start | bytes 1572872 | tf_op jit(solution)/shard_map/ppermute | solution.py:562
  85.6 2.3 %collective-permute-start.10 = (bf16[8,128,128]{2,1,0:T(8,128)(2,1)S(1)}, bf16[8,128,128]{2,1,0:T(8,128)(2,1)S(1)}, u32[]{:S(2)}, u32[]{:S(2)}) collective-permute-start(bf16[8,128,128]{2,1,0:T(8,128)(2,1)S(1)} %get-tuple-element.45), channel_id=1, source_target_pairs={{0,4},{4,0},{1,5},{5,1},{2,6},{6,2},{3,7},{7,3},{8,12},{12,8},{9,1... | collective-permute-start | bytes 786440 | tf_op jit(solution)/shard_map/ppermute | solution.py:563
  86.1 10.8 %collective-permute-start.4 = (bf16[8,128,128]{2,1,0:T(8,128)(2,1)S(1)}, bf16[8,128,128]{2,1,0:T(8,128)(2,1)S(1)}, u32[]{:S(2)}, u32[]{:S(2)}) collective-permute-start(bf16[8,128,128]{2,1,0:T(8,128)(2,1)S(1)} %get-tuple-element.38), channel_id=1, source_target_pairs={{0,16},{8,24},{16,0},{24,8},{1,17},{9,25},{17,1},{25,9},{2,18},{10... | collective-permute-start | bytes 786440 | tf_op jit(solution)/shard_map/ppermute | solution.py:522
  90.4 57.5 %copy-start.2 = (f32[1,128,512]{2,1,0:T(8,128)S(1)}, f32[1,128,512]{2,1,0:T(8,128)}, u32[]{:S(2)}) copy-start(f32[1,128,512]{2,1,0:T(8,128)} %param.9) | copy-start | bytes 786436
  90.4 21.5 %collective-permute-start.11 = (bf16[8,128,256]{2,1,0:T(8,128)(2,1)S(1)}, bf16[8,128,256]{2,1,0:T(8,128)(2,1)S(1)}, u32[]{:S(2)}, u32[]{:S(2)}) collective-permute-start(bf16[8,128,256]{2,1,0:T(8,128)(2,1)S(1)} %get-tuple-element.49), channel_id=1, source_target_pairs={{0,8},{8,16},{16,24},{24,0},{1,9},{9,17},{17,25},{25,1},{2,10},{10... | collective-permute-start | bytes 1572872 | tf_op jit(solution)/shard_map/ppermute | solution.py:522
  90.5 21.4 %collective-permute-start.12 = (bf16[8,128,256]{2,1,0:T(8,128)(2,1)S(1)}, bf16[8,128,256]{2,1,0:T(8,128)(2,1)S(1)}, u32[]{:S(2)}, u32[]{:S(2)}) collective-permute-start(bf16[8,128,256]{2,1,0:T(8,128)(2,1)S(1)} %get-tuple-element.50), channel_id=1, source_target_pairs={{0,16},{8,24},{16,0},{24,8},{1,17},{9,25},{17,1},{25,9},{2,18},{10... | collective-permute-start | bytes 1572872 | tf_op jit(solution)/shard_map/ppermute | solution.py:522
  92.2 26.2 %collective-permute-start.13 = (bf16[8,128,256]{2,1,0:T(8,128)(2,1)S(1)}, bf16[8,128,256]{2,1,0:T(8,128)(2,1)S(1)}, u32[]{:S(2)}, u32[]{:S(2)}) collective-permute-start(bf16[8,128,256]{2,1,0:T(8,128)(2,1)S(1)} %get-tuple-element.51), channel_id=1, source_target_pairs={{0,24},{8,0},{16,8},{24,16},{1,25},{9,1},{17,9},{25,17},{2,26},{10... | collective-permute-start | bytes 1572872 | tf_op jit(solution)/shard_map/ppermute | solution.py:522
  140.3 4.3 %collective-permute-start.14 = (f32[128,128]{1,0:T(8,128)S(1)}, f32[128,128]{1,0:T(8,128)S(1)}, u32[]{:S(2)}, u32[]{:S(2)}) collective-permute-start(f32[128,128]{1,0:T(8,128)S(1)} %get-tuple-element.54.refs_4_), channel_id=1, source_target_pairs={{0,1},{1,2},{2,3},{3,0},{4,5},{5,6},{6,7},{7,4},{8,9},{9,10},{10,1... | collective-permute-start | bytes 196616 | tf_op jit(solution)/shard_map/ppermute | solution.py:505
  142.1 5.8 %collective-permute-start.15 = (f32[128,128]{1,0:T(8,128)S(1)}, f32[128,128]{1,0:T(8,128)S(1)}, u32[]{:S(2)}, u32[]{:S(2)}) collective-permute-start(f32[128,128]{1,0:T(8,128)S(1)} %get-tuple-element.55.refs_5_), channel_id=1, source_target_pairs={{0,2},{1,3},{2,0},{3,1},{4,6},{5,7},{6,4},{7,5},{8,10},{9,11},{10,... | collective-permute-start | bytes 196616 | tf_op jit(solution)/shard_map/ppermute | solution.py:505

commit v3 on v1

--- a/solution.py
+++ b/solution.py
@@ -297,7 +297,8 @@
 
 
 def products_kernel(n, info_ref, *refs):
-    own, right, across, (right_ref, across_ref) = refs[:n], refs[n : 2 * n], refs[2 * n : -2], refs[-2:]
+    own, right, across, outs = refs[:n], refs[n : 2 * n], refs[2 * n : -4], refs[-4:]
+    right_ref, across_ref, right_send, across_send = outs
     half = across_ref.shape[0]
     nt = ((1,), (1,))
     for s in range(2):
@@ -306,12 +307,16 @@
             return jnp.concatenate([r[s * half + c] for r in group], axis=1)
 
         def step(c, carry):
-            right_ref[s * half + c] = dot_dims(joined(own, c), joined(right, c), nt)
+            product = dot_dims(joined(own, c), joined(right, c), nt)
+            right_ref[s * half + c] = product
+            right_send[s * half + c] = product.astype(BF16)
             return carry
 
         def step_across(c, carry):
             other = jnp.concatenate([r[c] for r in across], axis=1)
-            across_ref[c] = dot_dims(joined(own, c), other, nt)
+            product = dot_dims(joined(own, c), other, nt)
+            across_ref[c] = product
+            across_send[c] = product.astype(BF16)
             return carry
 
         lax.fori_loop(0, half, step, 0, unroll=4)
@@ -370,7 +375,7 @@
         @pl.when(lax.rem(p, 2) == core)
         def _():
             at = lax.div(p, 2)
-            acc[at, :, lanes] += widen(ref[c])
+            acc[at, :, lanes] += widen(ref[c]).astype(F32)
 
         return carry
 
@@ -542,15 +547,15 @@
     across.append(send(hop, 1))
     own_diag, *sends = after_scatter(scatter_diag_kernel, [diag, their_diag], BLK, "scatter_diag")
     got_diag = along_y(sends)
-    off_right, off_across = call(
+    off_right, off_across, send_right, send_across = call(
         functools.partial(products_kernel, len(own)),
         [at_row, *own, *right, *across],
-        [f32_out(count, BLK, BLK), f32_out(half, BLK, BLK)],
+        [out(n, BLK, BLK) for out in (f32_out, bf16_out) for n in (count, half)],
         name="products",
-        deps=[got_diag[0], got_diag[2]],
-    )
-    their_right = lax.ppermute(off_right, "core", ring(2, 1))
-    their_across = lax.ppermute(off_across, "core", ring(2, 1))
+        deps=got_diag,
+    )
+    their_right = lax.ppermute(send_right, "core", ring(2, 1))
+    their_across = lax.ppermute(send_across, "core", ring(2, 1))
     own_off, *sends = after_scatter(
         scatter_off_kernel, [off_right, off_across, their_right, their_across], 2 * BLK, "scatter_off"
     )

time: 149 us -> 152 us (1.020)
  waiting for transfers between devices: 27.6 us -> 30.2 us
    ppermute x6, waiting for transfers between devices: 16.1 us -> 19 us  [along_y(): return [lax.ppermute(s, 'y', ring(ny, d + 1)) for d, s in enumerate(sends)]]
  transfers between devices with their start and end apart: 17 -> 17, of which waited for: 9 -> 9; matrix products, arithmetic and copies ran while one was open for 0% -> 0% of each run, Pallas kernels for 17% -> 15%
where the time goes in v3:
time: 152 us
  blocking collectives  57.2 us (38%)
  Pallas kernels  45.4 us (30%)
  waiting for transfers between devices  30.2 us (20%)
  starting transfers between devices  16 us (11%)
  local copies, waits for them, and re-layouts  1.76 us (1%)
    all_to_all x2, blocking collectives, sum_y(): return (own, lax.all_to_all(sends, 'z', 0, 0, tiled=True))  35.3 us
    pallas_call x3, Pallas kernels, grid_call(): pl.pallas_call(kernel, grid=(1,), in_specs=in_specs, out_specs=[spec for...  30.6 us
    psum x1, blocking collectives, on_device(): known = lax.psum(known, COL)  21.9 us
    ppermute x6, waiting for transfers between devices, along_y(): return [lax.ppermute(s, 'y', ring(ny, d + 1)) for d, s in enumerate(sends)]  19 us
    pallas_call x9, Pallas kernels, call(): pl.pallas_call(body, in_specs=specs + [ANY_SPEC] * n_more, out_specs=[pl....  14.8 us
    ppermute x8, starting transfers between devices, send(): return lax.ppermute(blocks, 'row', ring(4, distance))  9.5 us
    ppermute x8, waiting for transfers between devices, send(): return lax.ppermute(blocks, 'row', ring(4, distance))  9.42 us
    ppermute x6, starting transfers between devices, along_y(): return [lax.ppermute(s, 'y', ring(ny, d + 1)) for d, s in enumerate(sends)]  5.91 us
  transfers between devices with their start and end apart: 17, of which 9 were waited for; matrix products, arithmetic and copies ran while one was open for 0% of the time, Pallas kernels for 15%

profile of v3, /device:TPU:26, one launch (start us, length us, event | category | flops | bytes accessed | tf_op | source)
XLA Modules:
  0.0 152.0 jit_solution(7537008385807801288)
XLA Ops:
  0.6 1.6 %copy-done.1 = f32[2,512,512]{2,1,0:T(8,128)S(1)} copy-done((f32[2,512,512]{2,1,0:T(8,128)S(1)}, f32[2,512,512]{2,1,0:T(8,128)}, u32[]{:S(2)}) %copy-start.1) | copy-done | bytes 2097176
  2.2 14.0 %first_chunk.1 = (f32[2,256,512]{2,1,0:T(8,128)S(1)}, f32[2,1024,512]{2,1,0:T(8,128)}, bf16[2,1024,256]{2,1,0:T(8,128)(2,1)S(1)}, bf16[1024,256]{1,0:T(8,128)(2,1)S(1)}) custom-call(s32[1]{0:T(128)} %bitcast.info_ref.refs_0_, f32[2,512,512]{2,1,0:T(8,128)S(1)} %copy-done.1, f32[2,1024,512]{2,1,0:T(8,128)} %bitcast.13), custom_call_target="tpu_custom_call" | custom-call | flops 1000000 | bytes 10000 | tf_op jit(solution)/shard_map/first_chunk/pallas_call | solution.py:206
  16.2 0.6 collective-permute-start.1
  16.9 1.5 collective-permute-start
  18.3 11.6 %second_factor.1.w_ref = f32[2,256,512]{2,1,0:T(8,128)S(1)} custom-call(f32[2,512,512]{2,1,0:T(8,128)S(1)} %copy-done.1, f32[2,256,512]{2,1,0:T(8,128)S(1)} %get-tuple-element.29.refs_0_), custom_call_target="tpu_custom_call" | custom-call | flops 1000000 | bytes 10000 | tf_op jit(solution)/shard_map/second_factor/pallas_call | solution.py:206
  29.9 1.4 collective-permute-done.refs_1_
  31.4 5.0 %second_chunk.1 = (f32[2,1024,512]{2,1,0:T(8,128)}, bf16[2,1024,256]{2,1,0:T(8,128)(2,1)}, bf16[1024,256]{1,0:T(8,128)(2,1)}, f32[16,128,128]{2,1,0:T(8,128)S(1)}, bf16[16,128,128]{2,1,0:T(8,128)(2,1)}) custom-call(s32[1]{0:T(128)} %bitcast.info_ref.refs_0_, f32[2,256,512]{2,1,0:T(8,128)S(1)} %second_factor.1.w_ref, ...), custom_call_target="tpu_custom_call", output_to_operand_aliasing={{0}: (4, {})} | custom-call | flops 1000000 | bytes 10000 | tf_op jit(solution)/shard_map/second_chunk/pallas_call | solution.py:206
  36.4 0.5 collective-permute-start.8
  36.8 2.5 %collective-permute-start.6 = (bf16[16,128,256]{2,1,0:T(8,128)(2,1)}, bf16[16,128,256]{2,1,0:T(8,128)(2,1)}, u32[]{:S(2)}, u32[]{:S(2)}) collective-permute-start(bf16[16,128,256]{2,1,0:T(8,128)(2,1)} %bitcast.10.refs_2_), channel_id=1, source_target_pairs={{0,3},{1,0},{2,1},{3,2},{4,7},{5,4},{6,5},{7,6},{8,11},{9,8},{10,9... | collective-permute-start | bytes 3145736 | tf_op jit(solution)/shard_map/ppermute | solution.py:499
  39.3 0.0 collective-permute-start.2
  39.3 0.1 reshape.36.refs_2_
  40.1 0.1 stack.20.refs_0_
  40.2 2.2 %collective-permute-done.1.refs_4_.refs_3_ = bf16[16,128,256]{2,1,0:T(8,128)(2,1)S(1)} collective-permute-done((bf16[16,128,256]{2,1,0:T(8,128)(2,1)S(1)}, bf16[16,128,256]{2,1,0:T(8,128)(2,1)S(1)}, u32[]{:S(2)}, u32[]{:S(2)}) %collective-permute-start.1) | collective-permute-done | bytes 1048608 | tf_op jit(solution)/shard_map/ppermute | solution.py:499
  42.4 0.6 known.1
  42.9 21.9 %psum.7.refs_1_ = s32[9,128]{1,0:T(8,128)S(1)} all-reduce(s32[9,128]{1,0:T(8,128)S(1)} %known.1), channel_id=1, replica_groups=mesh['z'=8,'y'=4,'core'=2,'row'=4] {'z','y','core'}, use_global_device_ids=true, to_apply=%region_0.0 | all-reduce | flops 1152 | bytes 9216 | tf_op jit(solution)/shard_map/psum | solution.py:545
  64.9 0.5 pass_on.1
  65.4 1.6 %collective-permute-start.9 = (bf16[8,128,256]{2,1,0:T(8,128)(2,1)}, bf16[8,128,256]{2,1,0:T(8,128)(2,1)S(1)}, u32[]{:S(2)}, u32[]{:S(2)}) collective-permute-start(bf16[8,128,256]{2,1,0:T(8,128)(2,1)} %pass_on.1), channel_id=1, source_target_pairs={{0,1},{1,2},{2,3},{3,0},{4,5},{5,6},{6,7},{7,4},{8,9},{9,10},{10,1... | collective-permute-start | bytes 1572872 | tf_op jit(solution)/shard_map/ppermute | solution.py:499
  67.0 0.0 collective-permute-done.2.refs_4_
  67.0 3.0 %scatter_diag.1 = (f32[8,128,128]{2,1,0:T(8,128)S(1)}, bf16[8,128,128]{2,1,0:T(8,128)(2,1)S(1)}, bf16[8,128,128]{2,1,0:T(8,128)(2,1)S(1)}, bf16[8,128,128]{2,1,0:T(8,128)(2,1)S(1)}) custom-call(s32[5]{0:T(128)S(1)} %stack.20.refs_0_, s32[9,128]{1,0:T(8,128)S(1)} %psum.7.refs_1_, s32[16]{0:T(128)S(1)} %reshape.36.refs_2_, ...), custom_call_target="tpu_custom_call" | custom-call | flops 1000000 | bytes 10000 | tf_op jit(solution)/shard_map/scatter_diag/pallas_call | solution.py:286
  70.0 2.7 %collective-permute-start.3 = (bf16[8,128,128]{2,1,0:T(8,128)(2,1)S(1)}, bf16[8,128,128]{2,1,0:T(8,128)(2,1)S(1)}, u32[]{:S(2)}, u32[]{:S(2)}) collective-permute-start(bf16[8,128,128]{2,1,0:T(8,128)(2,1)S(1)} %get-tuple-element.37), channel_id=1, source_target_pairs={{0,8},{8,16},{16,24},{24,0},{1,9},{9,17},{17,25},{25,1},{2,10},{10... | collective-permute-start | bytes 786440 | tf_op jit(solution)/shard_map/ppermute | solution.py:516
  72.7 0.0 collective-permute-start.4
  72.7 0.0 collective-permute-done.7.refs_5_
  72.7 1.1 collective-permute-start.5
  73.8 6.6 %collective-permute-done.3.refs_7_.refs_2_ = bf16[8,128,128]{2,1,0:T(8,128)(2,1)S(1)} collective-permute-done((bf16[8,128,128]{2,1,0:T(8,128)(2,1)S(1)}, bf16[8,128,128]{2,1,0:T(8,128)(2,1)S(1)}, u32[]{:S(2)}, u32[]{:S(2)}) %collective-permute-start.3) | collective-permute-done | bytes 262176 | tf_op jit(solution)/shard_map/ppermute | solution.py:516
  80.4 1.0 collective-permute-done.4.refs_8_.refs_3_
  81.5 2.4 %collective-permute-done.5.refs_9_.refs_4_ = bf16[8,128,128]{2,1,0:T(8,128)(2,1)S(1)} collective-permute-done((bf16[8,128,128]{2,1,0:T(8,128)(2,1)S(1)}, bf16[8,128,128]{2,1,0:T(8,128)(2,1)S(1)}, u32[]{:S(2)}, u32[]{:S(2)}) %collective-permute-start.5) | collective-permute-done | bytes 262176 | tf_op jit(solution)/shard_map/ppermute | solution.py:516
  83.8 0.0 collective-permute-done.9.refs_6_
  83.8 0.0 collective-permute-done.6.refs_4_
  83.8 3.5 %products.1 = (f32[16,128,128]{2,1,0:T(8,128)S(1)}, f32[8,128,128]{2,1,0:T(8,128)S(1)}, bf16[16,128,128]{2,1,0:T(8,128)(2,1)S(1)}, bf16[8,128,128]{2,1,0:T(8,128)(2,1)S(1)}) custom-call(s32[1]{0:T(128)} %bitcast.info_ref.refs_0_, bf16[16,128,256]{2,1,0:T(8,128)(2,1)S(1)} %bitcast.17, bf16[16,128,256]{2,1,0:T(8,128)(2,1)} %bitcast.10.refs_2_, ...), custom_call_target="tpu_custom_call" | custom-call | flops 1000000 | bytes 10000 | tf_op jit(solution)/shard_map/products/pallas_call | solution.py:286
  87.3 0.1 collective-permute-start.10
  87.4 0.5 collective-permute-start.11
  87.9 1.8 %collective-permute-done.11.refs_6_ = bf16[8,128,128]{2,1,0:T(8,128)(2,1)S(1)} collective-permute-done((bf16[8,128,128]{2,1,0:T(8,128)(2,1)S(1)}, bf16[8,128,128]{2,1,0:T(8,128)(2,1)S(1)}, u32[]{:S(2)}, u32[]{:S(2)}) %collective-permute-start.11) | collective-permute-done | bytes 262176 | tf_op jit(solution)/shard_map/ppermute | solution.py:558
  89.7 0.0 collective-permute-done.10.refs_5_
  89.7 2.5 %scatter_off.1 = (f32[8,128,256]{2,1,0:T(8,128)S(1)}, bf16[8,128,256]{2,1,0:T(8,128)(2,1)S(1)}, bf16[8,128,256]{2,1,0:T(8,128)(2,1)S(1)}, bf16[8,128,256]{2,1,0:T(8,128)(2,1)S(1)}) custom-call(s32[5]{0:T(128)S(1)} %stack.20.refs_0_, s32[9,128]{1,0:T(8,128)S(1)} %psum.7.refs_1_, s32[16]{0:T(128)S(1)} %reshape.36.refs_2_, ...), custom_call_target="tpu_custom_call" | custom-call | flops 1000000 | bytes 10000 | tf_op jit(solution)/shard_map/scatter_off/pallas_call | solution.py:286
  92.2 0.0 copy-start.2
  92.2 1.0 collective-permute-start.12
  93.2 0.2 collective-permute-start.13
  93.4 0.9 collective-permute-start.14
  94.3 1.8 %sum_diag.1 = (f32[128,128]{1,0:T(8,128)S(1)}, bf16[8,128,128]{2,1,0:T(8,128)(2,1)S(1)}) custom-call(s32[5]{0:T(128)S(1)} %stack.20.refs_0_, f32[8,128,128]{2,1,0:T(8,128)S(1)} %get-tuple-element.36.refs_1_, bf16[8,128,128]{2,1,0:T(8,128)(2,1)S(1)} %collective-permute-done.3.refs_7_.refs_2_, bf16[8,128,128]{2,1,0:T(8,128)(2,1)S(1)} %collective-permute-done.4.refs_8_.refs_3_, ...), custom_call_target="tpu_custom_call" | custom-call | flops 1000000 | bytes 10000 | tf_op jit(solution)/shard_map/sum_diag/pallas_call | solution.py:286
  96.1 14.6 %all_to_all.10.refs_5_.refs_3_ = bf16[8,128,128]{2,1,0:T(8,128)(2,1)S(1)} all-to-all(bf16[8,128,128]{2,1,0:T(8,128)(2,1)S(1)} %get-tuple-element.48), channel_id=1, replica_groups=mesh['z'=8,'y'=4,'core'=2,'row'=4] {'z'}, dimensions={0} | all-to-all | bytes 524288 | tf_op jit(solution)/shard_map/all_to_all | solution.py:523
  110.7 9.0 %collective-permute-done.14.refs_4_ = bf16[8,128,256]{2,1,0:T(8,128)(2,1)S(1)} collective-permute-done((bf16[8,128,256]{2,1,0:T(8,128)(2,1)S(1)}, bf16[8,128,256]{2,1,0:T(8,128)(2,1)S(1)}, u32[]{:S(2)}, u32[]{:S(2)}) %collective-permute-start.14) | collective-permute-done | bytes 524320 | tf_op jit(solution)/shard_map/ppermute | solution.py:516
  119.6 0.8 sum_off.1
  120.5 20.7 %all_to_all.11.refs_2_ = bf16[8,128,256]{2,1,0:T(8,128)(2,1)S(1)} all-to-all(bf16[8,128,256]{2,1,0:T(8,128)(2,1)S(1)} %get-tuple-element.53), channel_id=1, replica_groups=mesh['z'=8,'y'=4,'core'=2,'row'=4] {'z'}, dimensions={0} | all-to-all | bytes 1048576 | tf_op jit(solution)/shard_map/all_to_all | solution.py:523
  141.2 0.7 last_sum.1
  141.8 2.9 %collective-permute-start.15 = (f32[128,128]{1,0:T(8,128)S(1)}, f32[128,128]{1,0:T(8,128)S(1)}, u32[]{:S(2)}, u32[]{:S(2)}) collective-permute-start(f32[128,128]{1,0:T(8,128)S(1)} %get-tuple-element.54.refs_4_), channel_id=1, source_target_pairs={{0,1},{1,2},{2,3},{3,0},{4,5},{5,6},{6,7},{7,4},{8,9},{9,10},{10,1... | collective-permute-start | bytes 196616 | tf_op jit(solution)/shard_map/ppermute | solution.py:499
  144.7 1.9 %collective-permute-done.15.refs_6_ = f32[128,128]{1,0:T(8,128)S(1)} collective-permute-done((f32[128,128]{1,0:T(8,128)S(1)}, f32[128,128]{1,0:T(8,128)S(1)}, u32[]{:S(2)}, u32[]{:S(2)}) %collective-permute-start.15) | collective-permute-done | bytes 65568 | tf_op jit(solution)/shard_map/ppermute | solution.py:499
  146.6 3.8 %collective-permute-done.16.refs_7_ = f32[128,128]{1,0:T(8,128)S(1)} collective-permute-done((f32[128,128]{1,0:T(8,128)S(1)}, f32[128,128]{1,0:T(8,128)S(1)}, u32[]{:S(2)}, u32[]{:S(2)}) %collective-permute-start.16) | collective-permute-done | bytes 65568 | tf_op jit(solution)/shard_map/ppermute | solution.py:499
  150.5 1.5 finish.1
  (11 shorter events, 0.0 us)
Async XLA Ops:
  0.6 1.6 %copy-start.1 = (f32[2,512,512]{2,1,0:T(8,128)S(1)}, f32[2,512,512]{2,1,0:T(8,128)}, u32[]{:S(2)}) copy-start(f32[2,512,512]{2,1,0:T(8,128)} %diag_ref.3) | copy-start | bytes 6291460
  2.2 29.1 %copy-start = (f32[2,8,128,512]{3,2,1,0:T(8,128)S(1)}, f32[2,8,128,512]{3,2,1,0:T(8,128)}, u32[]{:S(2)}) copy-start(f32[2,8,128,512]{3,2,1,0:T(8,128)} %param.6) | copy-start | bytes 12582916
  16.2 26.1 %collective-permute-start.1 = (bf16[16,128,256]{2,1,0:T(8,128)(2,1)S(1)}, bf16[16,128,256]{2,1,0:T(8,128)(2,1)S(1)}, u32[]{:S(2)}, u32[]{:S(2)}) collective-permute-start(bf16[16,128,256]{2,1,0:T(8,128)(2,1)S(1)} %bitcast.15), channel_id=1, source_target_pairs={{0,3},{1,0},{2,1},{3,2},{4,7},{5,4},{6,5},{7,6},{8,11},{9,8},{10,9... | collective-permute-start | bytes 3145736 | tf_op jit(solution)/shard_map/ppermute | solution.py:499
  16.9 14.5 %collective-permute-start = (bf16[8,128,256]{2,1,0:T(8,128)(2,1)S(1)}, bf16[8,128,256]{2,1,0:T(8,128)(2,1)}, u32[]{:S(2)}, u32[]{:S(2)}) collective-permute-start(bf16[8,128,256]{2,1,0:T(8,128)(2,1)S(1)} %bitcast.19), channel_id=1, source_target_pairs={{0,1},{1,2},{2,3},{3,0},{4,5},{5,6},{6,7},{7,4},{8,9},{9,10},{10,1... | collective-permute-start | bytes 1572872 | tf_op jit(solution)/shard_map/ppermute | solution.py:499
  31.4 8.0 %copy-start.3 = (s32[2,8]{1,0:T(2,128)S(1)}, s32[2,8]{1,0:T(2,128)}, u32[]{:S(2)}) copy-start(s32[2,8]{1,0:T(2,128)} %param.7) | copy-start | bytes 196
  36.4 28.5 %collective-permute-start.8 = (bf16[8,128,256]{2,1,0:T(8,128)(2,1)}, bf16[8,128,256]{2,1,0:T(8,128)(2,1)}, u32[]{:S(2)}, u32[]{:S(2)}) collective-permute-start(bf16[8,128,256]{2,1,0:T(8,128)(2,1)} %bitcast.11), channel_id=1, source_target_pairs={{0,1},{1,2},{2,3},{3,0},{4,5},{5,6},{6,7},{7,4},{8,9},{9,10},{10,1... | collective-permute-start | bytes 1572872 | tf_op jit(solution)/shard_map/ppermute | solution.py:499
  36.8 47.0 %collective-permute-start.6 = (bf16[16,128,256]{2,1,0:T(8,128)(2,1)}, bf16[16,128,256]{2,1,0:T(8,128)(2,1)}, u32[]{:S(2)}, u32[]{:S(2)}) collective-permute-start(bf16[16,128,256]{2,1,0:T(8,128)(2,1)} %bitcast.10.refs_2_), channel_id=1, source_target_pairs={{0,3},{1,0},{2,1},{3,2},{4,7},{5,4},{6,5},{7,6},{8,11},{9,8},{10,9... | collective-permute-start | bytes 3145736 | tf_op jit(solution)/shard_map/ppermute | solution.py:499
  39.3 27.7 %collective-permute-start.2 = (bf16[16,128,128]{2,1,0:T(8,128)(2,1)}, bf16[16,128,128]{2,1,0:T(8,128)(2,1)}, u32[]{:S(2)}, u32[]{:S(2)}) collective-permute-start(bf16[16,128,128]{2,1,0:T(8,128)(2,1)} %get-tuple-element.35), channel_id=1, source_target_pairs={{0,4},{4,0},{1,5},{5,1},{2,6},{6,2},{3,7},{7,3},{8,12},{12,8},{9,1... | collective-permute-start | bytes 1572872 | tf_op jit(solution)/shard_map/ppermute | solution.py:535
  39.3 33.4 %collective-permute-start.7 = (bf16[8,128,256]{2,1,0:T(8,128)(2,1)}, bf16[8,128,256]{2,1,0:T(8,128)(2,1)}, u32[]{:S(2)}, u32[]{:S(2)}) collective-permute-start(bf16[8,128,256]{2,1,0:T(8,128)(2,1)} %collective-permute-done.refs_1_), channel_id=1, source_target_pairs={{0,1},{1,2},{2,3},{3,0},{4,5},{5,6},{6,7},{7,4},{8,9},{9,10},{10,1... | collective-permute-start | bytes 1572872 | tf_op jit(solution)/shard_map/ppermute | solution.py:499
  65.4 18.4 %collective-permute-start.9 = (bf16[8,128,256]{2,1,0:T(8,128)(2,1)}, bf16[8,128,256]{2,1,0:T(8,128)(2,1)S(1)}, u32[]{:S(2)}, u32[]{:S(2)}) collective-permute-start(bf16[8,128,256]{2,1,0:T(8,128)(2,1)} %pass_on.1), channel_id=1, source_target_pairs={{0,1},{1,2},{2,3},{3,0},{4,5},{5,6},{6,7},{7,4},{8,9},{9,10},{10,1... | collective-permute-start | bytes 1572872 | tf_op jit(solution)/shard_map/ppermute | solution.py:499
  70.0 10.4 %collective-permute-start.3 = (bf16[8,128,128]{2,1,0:T(8,128)(2,1)S(1)}, bf16[8,128,128]{2,1,0:T(8,128)(2,1)S(1)}, u32[]{:S(2)}, u32[]{:S(2)}) collective-permute-start(bf16[8,128,128]{2,1,0:T(8,128)(2,1)S(1)} %get-tuple-element.37), channel_id=1, source_target_pairs={{0,8},{8,16},{16,24},{24,0},{1,9},{9,17},{17,25},{25,1},{2,10},{10... | collective-permute-start | bytes 786440 | tf_op jit(solution)/shard_map/ppermute | solution.py:516
  72.7 8.8 %collective-permute-start.4 = (bf16[8,128,128]{2,1,0:T(8,128)(2,1)S(1)}, bf16[8,128,128]{2,1,0:T(8,128)(2,1)S(1)}, u32[]{:S(2)}, u32[]{:S(2)}) collective-permute-start(bf16[8,128,128]{2,1,0:T(8,128)(2,1)S(1)} %get-tuple-element.38), channel_id=1, source_target_pairs={{0,16},{8,24},{16,0},{24,8},{1,17},{9,25},{17,1},{25,9},{2,18},{10... | collective-permute-start | bytes 786440 | tf_op jit(solution)/shard_map/ppermute | solution.py:516
  72.7 11.1 %collective-permute-start.5 = (bf16[8,128,128]{2,1,0:T(8,128)(2,1)S(1)}, bf16[8,128,128]{2,1,0:T(8,128)(2,1)S(1)}, u32[]{:S(2)}, u32[]{:S(2)}) collective-permute-start(bf16[8,128,128]{2,1,0:T(8,128)(2,1)S(1)} %get-tuple-element.39), channel_id=1, source_target_pairs={{0,24},{8,0},{16,8},{24,16},{1,25},{9,1},{17,9},{25,17},{2,26},{10... | collective-permute-start | bytes 786440 | tf_op jit(solution)/shard_map/ppermute | solution.py:516
  87.3 2.4 %collective-permute-start.10 = (bf16[16,128,128]{2,1,0:T(8,128)(2,1)S(1)}, bf16[16,128,128]{2,1,0:T(8,128)(2,1)S(1)}, u32[]{:S(2)}, u32[]{:S(2)}) collective-permute-start(bf16[16,128,128]{2,1,0:T(8,128)(2,1)S(1)} %get-tuple-element.44), channel_id=1, source_target_pairs={{0,4},{4,0},{1,5},{5,1},{2,6},{6,2},{3,7},{7,3},{8,12},{12,8},{9,1... | collective-permute-start | bytes 1572872 | tf_op jit(solution)/shard_map/ppermute | solution.py:557
  87.4 2.3 %collective-permute-start.11 = (bf16[8,128,128]{2,1,0:T(8,128)(2,1)S(1)}, bf16[8,128,128]{2,1,0:T(8,128)(2,1)S(1)}, u32[]{:S(2)}, u32[]{:S(2)}) collective-permute-start(bf16[8,128,128]{2,1,0:T(8,128)(2,1)S(1)} %get-tuple-element.45), channel_id=1, source_target_pairs={{0,4},{4,0},{1,5},{5,1},{2,6},{6,2},{3,7},{7,3},{8,12},{12,8},{9,1... | collective-permute-start | bytes 786440 | tf_op jit(solution)/shard_map/ppermute | solution.py:558
  92.2 58.3 %copy-start.2 = (f32[1,128,512]{2,1,0:T(8,128)S(1)}, f32[1,128,512]{2,1,0:T(8,128)}, u32[]{:S(2)}) copy-start(f32[1,128,512]{2,1,0:T(8,128)} %param.9) | copy-start | bytes 786436
  92.2 18.5 %collective-permute-start.12 = (bf16[8,128,256]{2,1,0:T(8,128)(2,1)S(1)}, bf16[8,128,256]{2,1,0:T(8,128)(2,1)S(1)}, u32[]{:S(2)}, u32[]{:S(2)}) collective-permute-start(bf16[8,128,256]{2,1,0:T(8,128)(2,1)S(1)} %get-tuple-element.49), channel_id=1, source_target_pairs={{0,8},{8,16},{16,24},{24,0},{1,9},{9,17},{17,25},{25,1},{2,10},{10... | collective-permute-start | bytes 1572872 | tf_op jit(solution)/shard_map/ppermute | solution.py:516
  93.2 17.5 %collective-permute-start.13 = (bf16[8,128,256]{2,1,0:T(8,128)(2,1)S(1)}, bf16[8,128,256]{2,1,0:T(8,128)(2,1)S(1)}, u32[]{:S(2)}, u32[]{:S(2)}) collective-permute-start(bf16[8,128,256]{2,1,0:T(8,128)(2,1)S(1)} %get-tuple-element.50), channel_id=1, source_target_pairs={{0,16},{8,24},{16,0},{24,8},{1,17},{9,25},{17,1},{25,9},{2,18},{10... | collective-permute-start | bytes 1572872 | tf_op jit(solution)/shard_map/ppermute | solution.py:516
  93.4 26.2 %collective-permute-start.14 = (bf16[8,128,256]{2,1,0:T(8,128)(2,1)S(1)}, bf16[8,128,256]{2,1,0:T(8,128)(2,1)S(1)}, u32[]{:S(2)}, u32[]{:S(2)}) collective-permute-start(bf16[8,128,256]{2,1,0:T(8,128)(2,1)S(1)} %get-tuple-element.51), channel_id=1, source_target_pairs={{0,24},{8,0},{16,8},{24,16},{1,25},{9,1},{17,9},{25,17},{2,26},{10... | collective-permute-start | bytes 1572872 | tf_op jit(solution)/shard_map/ppermute | solution.py:516
  141.8 4.8 %collective-permute-start.15 = (f32[128,128]{1,0:T(8,128)S(1)}, f32[128,128]{1,0:T(8,128)S(1)}, u32[]{:S(2)}, u32[]{:S(2)}) collective-permute-start(f32[128,128]{1,0:T(8,128)S(1)} %get-tuple-element.54.refs_4_), channel_id=1, source_target_pairs={{0,1},{1,2},{2,3},{3,0},{4,5},{5,6},{6,7},{7,4},{8,9},{9,10},{10,1... | collective-permute-start | bytes 196616 | tf_op jit(solution)/shard_map/ppermute | solution.py:499
  144.7 5.8 %collective-permute-start.16 = (f32[128,128]{1,0:T(8,128)S(1)}, f32[128,128]{1,0:T(8,128)S(1)}, u32[]{:S(2)}, u32[]{:S(2)}) collective-permute-start(f32[128,128]{1,0:T(8,128)S(1)} %get-tuple-element.55.refs_5_), channel_id=1, source_target_pairs={{0,2},{1,3},{2,0},{3,1},{4,6},{5,7},{6,4},{7,5},{8,10},{9,11},{10,... | collective-permute-start | bytes 196616 | tf_op jit(solution)/shard_map/ppermute | solution.py:499
